TPU v7x, 32 devices: a whole 2x2x4 slice. The times are simulated.
32 devices in a mesh: dp: 4 (over y, core), seq: 8 (over z, x).
Axes of the slice: x: 2, y: 2, z: 4, core: 2. Of those that a mesh axis runs over, the one named last changes fastest.
Arguments:
- tokens: bfloat16 [8192, 640], P(('dp', 'seq')), may hold values from -6 to 6
- positions: int32 [8192], P(('dp', 'seq')), may hold values from 0 to 2047, as said below
- cotangent: bfloat16 [8192, 640], P(('dp', 'seq')), may hold values from -6 to 6
- w_query: bfloat16 [655360], P(('dp', 'seq')), may hold values from -0.25 to 0.25
- w_key: bfloat16 [163840], P(('dp', 'seq')), may hold values from -0.25 to 0.25
- w_value: bfloat16 [163840], P(('dp', 'seq')), may hold values from -0.25 to 0.25
- w_out: bfloat16 [655360], P(('dp', 'seq')), may hold values from -0.1875 to 0.1875
- w_gate: bfloat16 [1310720], P(('dp', 'seq')), may hold values from -0.25 to 0.25
- w_up: bfloat16 [1310720], P(('dp', 'seq')), may hold values from -0.25 to 0.25
- w_down: bfloat16 [1310720], P(('dp', 'seq')), may hold values from -0.125 to 0.125
- gains: bfloat16 [3072], P(('dp', 'seq')), may hold values from 0.099609375 to 1.8984375
Outputs:
- layer_out: bfloat16 [8192, 640], P(('dp', 'seq'))
- input_grad: float32 [8192, 640], P(('dp', 'seq'))
- grad_query: float32 [655360], P(('dp', 'seq'))
- grad_key: float32 [163840], P(('dp', 'seq'))
- grad_value: float32 [163840], P(('dp', 'seq'))
- grad_out: float32 [655360], P(('dp', 'seq'))
- grad_gate: float32 [1310720], P(('dp', 'seq'))
- grad_up: float32 [1310720], P(('dp', 'seq'))
- grad_down: float32 [1310720], P(('dp', 'seq'))
- grad_gains: float32 [3072], P(('dp', 'seq'))
Inputs may be any that keep to these rules, and one draw needn't show every extreme that they name: Each of the 4 sequences of 2048 tokens (token t belongs to sequence t // 2048) is cut into one to three contiguous documents; positions count 0, 1, 2, ... from each document's first token. One document of each sequence begins within the sequence's first half of 256 tokens and ends within its last half of 256 tokens. One sequence is a single document.
All inputs are finite; a program needn't handle non-finite values.
Results may differ from a plain program's by a relative error of at most 0.017.
Values may be sent and summed in bfloat16 or wider, within the bound.
No kernel may reach another device: no remote copies, remote signals or barrier semaphores. Data moves between devices by JAX's collectives and lax.ppermute only.
A program may use at most 128 MiB of HBM per device.

v0:
```python
import functools
import numpy as np
import jax
import jax.numpy as jnp
from jax import lax
from jax.experimental import pallas as pl
from jax.experimental.pallas import tpu as pltpu
from jax.sharding import PartitionSpec as P

D = 640
HEADS = 4
HD = 256
FF = 2048
WIN = 512
BLK = 256
BACK = 2
AXES = ("dp", "seq")
F32 = jnp.float32
BF16 = jnp.bfloat16
QW = HEADS * HD
SPAN = (BACK + 1) * BLK

PARTS = 32
MAIN = 16
DEPTH = PARTS * MAIN
HALF = DEPTH // 2
LANES = 128
ATTN_A = QW + QW // 4 + LANES
ATTN_B = 2 * HD + HD // 2 + 2 * D
FFN_A = FF + FF // 4 + 2 * D
Z_BITS = (1, 2)
LOW, CORE, HIGH = 0, 3, 4
ORDER_A = (LOW, HIGH, CORE)
ORDER_B = (HIGH, LOW, CORE)

epsilon = 1e-06
lowest = -1e30


def slot_shards(order):
    shards = np.arange(4, dtype=np.int32) << Z_BITS[0]
    for bit in order:
        shards = np.concatenate([shards, shards ^ (1 << bit)])
    return shards


SLOTS_A = slot_shards(ORDER_A)
SLOTS_B = slot_shards(ORDER_B)


def extra_bits():
    return (lax.axis_size("dp") * lax.axis_size("seq")).bit_length() - PARTS.bit_length()


def exchanged(value, mask):
    count = lax.axis_size("dp") * lax.axis_size("seq")
    return lax.ppermute(value, AXES, [(i, i ^ mask) for i in range(count)])


def exchanged_part(value, mask):
    return exchanged(value, mask << extra_bits())


def passed_along(value, axis, steps):
    count = lax.axis_size(axis)
    first, last = (max(0, -steps), min(count, count - steps))
    return lax.ppermute(value, axis, [(source, source + steps) for source in range(first, last)])


def dot(left, right, left_dim=1, right_dim=0):
    return lax.dot_general(
        left, right, (((left_dim,), (right_dim,)), ((), ())), preferred_element_type=F32
    )


def unit_of(values):
    inverse = lax.rsqrt(jnp.mean(values * values, axis=-1, keepdims=True) + epsilon)
    return values * inverse, inverse


def rms_values_grad(incoming, unit_rows, inverse, gain_row):
    scaled = incoming * gain_row
    return inverse * (scaled - unit_rows * jnp.mean(scaled * unit_rows, axis=-1, keepdims=True))


def rotate(values, cos_rows, sin_rows):
    middle_at = values.shape[-1] // 2
    first_half = values[..., :middle_at]
    second_half = values[..., middle_at:]
    return jnp.concatenate(
        [
            first_half * cos_rows - second_half * sin_rows,
            second_half * cos_rows + first_half * sin_rows,
        ],
        axis=-1,
    )


def row_sum(values):
    return jnp.sum(values, axis=0, keepdims=True)


def column(index):
    return pl.ds(index * LANES, LANES)


def pack_kernel(
    query, key, value, out, gate, up, down, gains, attn, ffn, wide, quarter
):
    def load(source):
        rows = source.shape[0]
        wide[:rows, :] = source[...].astype(F32)

    def put_main(target, at, blocks, block):
        target[:, pl.ds(at, LANES)] = wide[pl.ds(block, MAIN, stride=blocks), :].astype(BF16)

    def put_tail(row, at, blocks, block):
        quarter[4 * row : 4 * row + 4, pl.ds(at, LANES)] = wide[
            pl.ds(MAIN * blocks + block, 4, stride=blocks), :
        ]

    def put_matrix(source, target, at):
        load(source)
        blocks = source.shape[0] // 20
        for block in range(blocks):
            put_main(target, at + block * LANES, blocks, block)
            each = blocks // 4
            put_tail(block // each, block % each * LANES, blocks, block)
        width = blocks * LANES // 4
        target[:, pl.ds(at + blocks * LANES, width)] = quarter[:, :width].astype(BF16)

    def put_groups(target, at, groups):
        blocks = D // LANES
        for place, group in enumerate(groups):
            for block in range(blocks):
                target[:, pl.ds(at + place * D + block * LANES, LANES)] = wide[
                    pl.ds(group * MAIN * blocks + block, MAIN, stride=blocks), :
                ].astype(BF16)

    put_matrix(query, attn, 0)
    attn[:, pl.ds(QW + QW // 4, LANES)] = gains[...]
    for place, source in enumerate((key, value)):
        load(source)
        for block in range(2):
            put_main(attn, ATTN_A + place * HD + block * LANES, 2, block)
            put_tail(2 * place + block, 0, 2, block)
    attn[:, pl.ds(ATTN_A + 2 * HD, LANES)] = quarter[:, :LANES].astype(BF16)
    load(out)
    put_groups(attn, ATTN_A + 2 * HD + HD // 2, (0, 1))
    put_matrix(gate, ffn, 0)
    put_matrix(up, ffn, FFN_A)
    load(down)
    put_groups(ffn, FF + FF // 4, (0, 1))
    put_groups(ffn, FFN_A + FF + FF // 4, (2, 3))


def unpack_matrix(source, at, target):
    blocks = target.shape[0] // 20
    each = blocks // 4
    tail_at = at + blocks * LANES
    for block in range(blocks):
        target[pl.ds(block, MAIN, stride=blocks), :] = source[:, pl.ds(at + block * LANES, LANES)]
        row = block // each * 4
        target[pl.ds(MAIN * blocks + block, 4, stride=blocks), :] = source[
            row : row + 4, pl.ds(tail_at + block % each * LANES, LANES)
        ]


def unpack_groups(source, at, target, groups):
    blocks = D // LANES
    for place, group in enumerate(groups):
        for block in range(blocks):
            target[pl.ds(group * MAIN * blocks + block, MAIN, stride=blocks), :] = source[
                :, pl.ds(at + place * D + block * LANES, LANES)
            ]


def unpack_ffn_kernel(part_a, part_b, gate, up, down):
    unpack_matrix(part_a, 0, gate)
    unpack_matrix(part_b, 0, up)
    unpack_groups(part_a, FF + FF // 4, down, (0, 1))
    unpack_groups(part_b, FF + FF // 4, down, (2, 3))


def unpack_attn_kernel(query_part, out_part, kv_part, query, key, value, out):
    unpack_matrix(query_part, 0, query)
    unpack_groups(out_part, 0, out, (0, 1))
    for place, target in enumerate((key, value)):
        for block in range(2):
            target[pl.ds(block, MAIN, stride=2), :] = kv_part[
                :, pl.ds(place * HD + block * LANES, LANES)
            ]
            row = 4 * (2 * place + block)
            target[pl.ds(2 * MAIN + block, 4, stride=2), :] = kv_part[
                row : row + 4, pl.ds(2 * HD, LANES)
            ]


def quarter_rows(tail_rows, quarter):
    lane = lax.broadcasted_iota(jnp.int32, tail_rows.shape, 1)
    return jnp.where(lane // 4 % 4 == quarter, tail_rows, jnp.zeros_like(tail_rows))


def packed_product(rows, mine, other, main_at, tail_at, quarter, width):
    tail = quarter_rows(rows[:, DEPTH:], quarter)
    main_at, tail_at = pl.ds(main_at, width), pl.ds(tail_at, width)
    return (
        dot(rows[:, :HALF], mine[:, main_at])
        + dot(rows[:, HALF:DEPTH], other[:, main_at])
        + dot(tail[:, :HALF], mine[:, tail_at])
        + dot(tail[:, HALF:], other[:, tail_at])
    )


def packed_back(incoming, mine, other, main_at, tail_at, quarter):
    width = incoming.shape[1]
    main_at, tail_at = pl.ds(main_at, width), pl.ds(tail_at, width)
    tail = jnp.concatenate(
        [dot(incoming, mine[:, tail_at], 1, 1), dot(incoming, other[:, tail_at], 1, 1)], axis=1
    )
    return jnp.concatenate(
        [
            dot(incoming, mine[:, main_at], 1, 1),
            dot(incoming, other[:, main_at], 1, 1),
            quarter_rows(tail, quarter),
        ],
        axis=1,
    )


def packed_grad(rows, incoming, keep, send, main_at):
    grad = dot(rows, incoming, 0, 0).astype(BF16)
    main_at = pl.ds(main_at, incoming.shape[1])
    keep[:, main_at] = grad[:HALF]
    send[:, main_at] = grad[HALF:]


def natural_columns(permuted, permutation):
    high = permuted.astype(BF16)
    low = (permuted - high.astype(F32)).astype(BF16)
    return dot(high, permutation, 1, 1) + dot(low, permutation, 1, 1)


def place_groups(target, me, slots, mine, other, at, groups, count):
    for slot in range(PARTS):
        source = mine if slot < PARTS // 2 else other
        row = slot % (PARTS // 2) * MAIN
        first = (me ^ int(slots[slot])) * (count * MAIN)
        for place, group in enumerate(groups):
            rows = pl.ds(pl.multiple_of(first + group * MAIN, MAIN), MAIN)
            target[rows, :] = source[row : row + MAIN, pl.ds(at + place * D, D)]


def take_groups(whole, me, slots, keep, send, at, groups, count):
    for slot in range(PARTS):
        target = keep if slot < PARTS // 2 else send
        row = slot % (PARTS // 2) * MAIN
        first = (me ^ int(slots[slot])) * (count * MAIN)
        for place, group in enumerate(groups):
            rows = pl.ds(pl.multiple_of(first + group * MAIN, MAIN), MAIN)
            target[row : row + MAIN, pl.ds(at + place * D, D)] = whole[rows, :]


def qkv_kernel(
    tokens, gain_d, gain_h, perm_a, perm_b, mine_a, other_a, mine_b, other_b, cos, sin,
    query_low, kv_low, query_raw, key_raw, rows_a, rows_b,
):
    unit, _ = unit_of(tokens[...].astype(F32))
    normed = (unit * gain_d[0:1, :]).astype(BF16)
    rows_a[...] = dot(normed, perm_a[...]).astype(BF16)
    rows_b[...] = dot(normed, perm_b[...]).astype(BF16)
    cos_rows, sin_rows = cos[...], sin[...]
    for head in range(HEADS):
        raw = packed_product(rows_a, mine_a, other_a, head * HD, QW, head, HD)
        at = pl.ds(head * HD, HD)
        query_raw[:, at] = raw
        normed_raw = unit_of(raw)[0] * gain_h[0:1, :]
        query_low[:, at] = (rotate(normed_raw, cos_rows, sin_rows) * HD**-0.5).astype(BF16)
    kv = [
        packed_product(rows_b, mine_b, other_b, c * LANES, 2 * HD, c, LANES) for c in range(4)
    ]
    raw = jnp.concatenate(kv[:2], axis=1)
    key_raw[...] = raw
    kv_low[:, :HD] = rotate(unit_of(raw)[0] * gain_h[1:2, :], cos_rows, sin_rows).astype(BF16)
    kv_low[:, HD:] = jnp.concatenate(kv[2:], axis=1).astype(BF16)


def allowed_pairs(block_index, positions):
    query_index = block_index * BLK + lax.broadcasted_iota(jnp.int32, (BLK, SPAN), 0)
    key_index = (block_index - BACK) * BLK + lax.broadcasted_iota(jnp.int32, (BLK, SPAN), 1)
    return (
        (key_index <= query_index)
        & (key_index > query_index - WIN)
        & (key_index >= query_index - positions[...])
    )


def attend_kernel(
    where, tokens, positions, gain_d, perm_a, perm_b, mine_b, other_b, query_low, kv_all,
    heads_out, log_total, attn_proj, middle, rows_a, rows_b, out_w,
):
    place_groups(out_w, where[0], SLOTS_B, mine_b, other_b, 2 * HD + HD // 2, (0, 1), 2)
    allowed = allowed_pairs(where[1], positions)
    for head in range(HEADS):
        at = pl.ds(head * HD, HD)
        scores = dot(query_low[:, at], kv_all[:, :HD], 1, 1)
        scores = jnp.where(allowed, scores, lowest)
        row_max = jnp.max(scores, axis=-1, keepdims=True)
        expo = jnp.exp(scores - row_max)
        total = jnp.sum(expo, axis=-1, keepdims=True)
        log_total[:, column(head)] = jnp.broadcast_to(row_max + jnp.log(total), (BLK, LANES))
        probs = (expo * (1.0 / total)).astype(BF16)
        heads_out[:, at] = dot(probs, kv_all[:, HD:]).astype(BF16)
    proj = dot(heads_out[...], out_w[...])
    attn_proj[...] = proj
    mid = tokens[...].astype(F32) + unit_of(proj)[0] * gain_d[1:2, :]
    middle[...] = mid
    normed = (unit_of(mid)[0] * gain_d[2:3, :]).astype(BF16)
    rows_a[...] = dot(normed, perm_a[...]).astype(BF16)
    rows_b[...] = dot(normed, perm_b[...]).astype(BF16)


TILE = 256
TILES = FF // TILE
TANH_SCALE = float(np.sqrt(2.0 / np.pi))


def ffn_kernel(
    where, middle, cotangent, gain_d, perm_a, perm_b, rows_a, rows_b, mine_a, other_a, mine_b,
    other_b, layer_out, keep_a, send_a, keep_b, send_b, mid_grad, gain_grad,
    down_w, down_grad, gate_s, up_s, hidden_s, gate_g, up_g, back_a, back_b,
):
    me = where[0]
    down_at = FF + FF // 4
    place_groups(down_w, me, SLOTS_A, mine_a, other_a, down_at, (0, 1), 4)
    place_groups(down_w, me, SLOTS_B, mine_b, other_b, down_at, (2, 3), 4)

    def tile_places(tile):
        at = pl.multiple_of(tile * TILE, TILE)
        tail_at = pl.multiple_of(FF + tile % 2 * TILE, TILE)
        return at, tail_at, tile // 2

    @pl.loop(0, TILES)
    def forward(tile):
        at, tail_at, quarter = tile_places(tile)
        gate = packed_product(rows_a, mine_a, other_a, at, tail_at, quarter, TILE)
        up = packed_product(rows_b, mine_b, other_b, at, tail_at, quarter, TILE)
        gate_s[:, pl.ds(at, TILE)] = gate
        up_s[:, pl.ds(at, TILE)] = up
        tanh = jnp.tanh(TANH_SCALE * (gate + 0.044715 * gate * gate * gate))
        hidden_s[:, pl.ds(at, TILE)] = (0.5 * gate * (1.0 + tanh) * up).astype(BF16)

    proj = dot(hidden_s[...], down_w[...])
    mid = middle[...]
    unit, inverse = unit_of(proj)
    layer_out[...] = (mid + unit * gain_d[3:4, :]).astype(BF16)
    out_grad = cotangent[...].astype(F32)
    gain_grad[0:1, :] = row_sum(out_grad * unit)
    proj_grad = rms_values_grad(out_grad, unit, inverse, gain_d[3:4, :]).astype(BF16)
    back_a[...] = jnp.zeros_like(back_a)
    back_b[...] = jnp.zeros_like(back_b)

    @pl.loop(0, TILES)
    def backward(tile):
        at, tail_at, quarter = tile_places(tile)
        cols = pl.ds(at, TILE)
        hidden_grad = dot(proj_grad, down_w[cols, :], 1, 1)
        down_grad[cols, :] = dot(hidden_s[:, cols], proj_grad, 0, 0).astype(BF16)
        gate, up = gate_s[:, cols], up_s[:, cols]
        square = gate * gate
        tanh = jnp.tanh(TANH_SCALE * (gate + 0.044715 * gate * square))
        slope = 0.5 * (1.0 + tanh) + 0.5 * gate * (1.0 - tanh * tanh) * TANH_SCALE * (
            1.0 + 3.0 * 0.044715 * square
        )
        gate_grad = (hidden_grad * up * slope).astype(BF16)
        up_grad = (hidden_grad * (0.5 * gate * (1.0 + tanh))).astype(BF16)
        gate_g[:, cols] = gate_grad
        up_g[:, cols] = up_grad
        back_a[...] += packed_back(gate_grad, mine_a, other_a, at, tail_at, quarter)
        back_b[...] += packed_back(up_grad, mine_b, other_b, at, tail_at, quarter)
        packed_grad(rows_a[:, :DEPTH], gate_grad, keep_a, send_a, at)
        packed_grad(rows_b[:, :DEPTH], up_grad, keep_b, send_b, at)

    for rows, grad_s, keep, send in ((rows_a, gate_g, keep_a, send_a), (rows_b, up_g, keep_b, send_b)):

        @pl.loop(0, 2)
        def tails(half):
            total = jnp.zeros((DEPTH, TILE), F32)
            for quarter in range(4):
                at = pl.multiple_of(quarter * (FF // 4) + half * TILE, TILE)
                total += dot(quarter_rows(rows[:, DEPTH:], quarter), grad_s[:, pl.ds(at, TILE)], 0, 0)
            at = pl.ds(pl.multiple_of(FF + half * TILE, TILE), TILE)
            keep[:, at] = total[:HALF].astype(BF16)
            send[:, at] = total[HALF:].astype(BF16)

    take_groups(down_grad, me, SLOTS_A, keep_a, send_a, down_at, (0, 1), 4)
    take_groups(down_grad, me, SLOTS_B, keep_b, send_b, down_at, (2, 3), 4)
    normed_grad = natural_columns(back_a[...], perm_a[...]) + natural_columns(
        back_b[...], perm_b[...]
    )
    unit, inverse = unit_of(mid)
    gain_grad[1:2, :] = row_sum(normed_grad * unit)
    mid_grad[...] = out_grad + rms_values_grad(normed_grad, unit, inverse, gain_d[2:3, :])


def attend_back_kernel(
    where, mid_grad, attn_proj, positions, gain_d, gain_h, out_w, heads_out, query_low, kv_all,
    log_total, query_raw, cos, sin, rows_a, mine_a, other_a,
    kv_earlier, kv_own, query_keep, query_send, out_keep, out_send, back_a, gain_grad_d,
    gain_grad_h, out_grad_s, kv_grad, query_grad_s,
):
    incoming = mid_grad[...]
    unit, inverse = unit_of(attn_proj[...])
    gain_grad_d[0:1, :] = row_sum(incoming * unit)
    proj_grad = rms_values_grad(incoming, unit, inverse, gain_d[1:2, :]).astype(BF16)
    for head in range(HEADS):
        at = pl.ds(head * HD, HD)
        out_grad_s[at, :] = dot(heads_out[:, at], proj_grad, 0, 0).astype(BF16)
    take_groups(out_grad_s, where[0], SLOTS_B, out_keep, out_send, 0, (0, 1), 2)
    allowed = allowed_pairs(where[1], positions)
    cos_rows, sin_rows = cos[...], sin[...]
    total_a = jnp.zeros((BLK, 2 * DEPTH), F32)
    gain_total = jnp.zeros((1, HD), F32)
    keys_grad = jnp.zeros((SPAN, HD), F32)
    values_grad = jnp.zeros((SPAN, HD), F32)
    for head in range(HEADS):
        at = pl.ds(head * HD, HD)
        heads_grad = dot(proj_grad, out_w[at, :], 1, 1).astype(BF16)
        scores = dot(query_low[:, at], kv_all[:, :HD], 1, 1)
        log_rows = log_total[:, pl.ds(head * LANES, 1)]
        probs = jnp.where(allowed, jnp.exp(jnp.where(allowed, scores - log_rows, 0.0)), 0.0)
        prob_grad = dot(heads_grad, kv_all[:, HD:], 1, 1)
        delta = jnp.sum(probs * prob_grad, axis=-1, keepdims=True)
        score_grad = (probs * (prob_grad - delta)).astype(BF16)
        keys_grad += dot(score_grad, query_low[:, at], 0, 0)
        values_grad += dot(probs.astype(BF16), heads_grad, 0, 0)
        query_grad = dot(score_grad, kv_all[:, :HD]) * HD**-0.5
        query_rot = rotate(query_grad, cos_rows, -sin_rows)
        unit, inverse = unit_of(query_raw[:, at])
        gain_total += row_sum(query_rot * unit)
        raw_grad = rms_values_grad(query_rot, unit, inverse, gain_h[0:1, :]).astype(BF16)
        query_grad_s[:, at] = raw_grad
        total_a += packed_back(raw_grad, mine_a, other_a, head * HD, QW, head)
        packed_grad(rows_a[:, :DEPTH], raw_grad, query_keep, query_send, head * HD)
    gain_grad_h[0:1, :] = gain_total
    kv_grad[:, :HD] = keys_grad
    kv_grad[:, HD:] = values_grad
    kv_earlier[...] = kv_grad[: BACK * BLK, :].astype(BF16)
    kv_own[...] = kv_grad[BACK * BLK :, :]
    back_a[...] = total_a
    tail = jnp.zeros((DEPTH, HD), F32)
    for head in range(HEADS):
        tail += dot(
            quarter_rows(rows_a[:, DEPTH:], head), query_grad_s[:, pl.ds(head * HD, HD)], 0, 0
        )
    query_keep[:, pl.ds(QW, HD)] = tail[:HALF].astype(BF16)
    query_send[:, pl.ds(QW, HD)] = tail[HALF:].astype(BF16)


def input_kernel(
    tokens, mid_grad, gain_d, gain_h, perm_a, perm_b, rows_b, mine_b, other_b, kv_own, came_one,
    came_two, key_raw, cos, sin, back_a, input_grad, kv_keep, kv_send, gain_grad_d, gain_grad_h,
):
    total = kv_own[...] + came_one[...].astype(F32) + came_two[...].astype(F32)
    key_rot = rotate(total[:, :HD], cos[...], -sin[...])
    unit, inverse = unit_of(key_raw[...])
    gain_grad_h[0:1, :] = row_sum(key_rot * unit)
    key_grad = rms_values_grad(key_rot, unit, inverse, gain_h[1:2, :]).astype(BF16)
    raw_grad = jnp.concatenate([key_grad, total[:, HD:].astype(BF16)], axis=1)
    back_b = jnp.zeros((BLK, 2 * DEPTH), F32)
    tail = jnp.zeros((DEPTH, LANES), F32)
    for c in range(4):
        part = raw_grad[:, c * LANES : (c + 1) * LANES]
        back_b += packed_back(part, mine_b, other_b, c * LANES, 2 * HD, c)
        tail += dot(quarter_rows(rows_b[:, DEPTH:], c), part, 0, 0)
    packed_grad(rows_b[:, :DEPTH], raw_grad, kv_keep, kv_send, 0)
    kv_keep[:, pl.ds(2 * HD, LANES)] = tail[:HALF].astype(BF16)
    kv_send[:, pl.ds(2 * HD, LANES)] = tail[HALF:].astype(BF16)
    normed_grad = natural_columns(back_a[...], perm_a[...]) + natural_columns(
        back_b, perm_b[...]
    )
    unit, inverse = unit_of(tokens[...].astype(F32))
    gain_grad_d[0:1, :] = row_sum(normed_grad * unit)
    input_grad[...] = mid_grad[...] + rms_values_grad(
        normed_grad, unit, inverse, gain_d[0:1, :]
    )


VMEM_LIMIT = 56 * 1024 * 1024


def call(kernel, outs, args, scratch=(), scalars=0, flops=0):
    vmem = pl.BlockSpec(memory_space=pltpu.VMEM)
    shapes = [jax.ShapeDtypeStruct(shape, kind) for shape, kind in outs]
    return pl.pallas_call(
        kernel,
        out_shape=shapes,
        in_specs=[pl.BlockSpec(memory_space=pltpu.SMEM)] * scalars + [vmem] * (len(args) - scalars),
        out_specs=[vmem] * len(outs),
        scratch_shapes=[pltpu.VMEM(shape, kind) for shape, kind in scratch],
        compiler_params=pltpu.CompilerParams(vmem_limit_bytes=VMEM_LIMIT),
        cost_estimate=pl.CostEstimate(flops=int(flops), bytes_accessed=0, transcendentals=0),
    )(*args)


def together(*values):
    return lax.optimization_barrier(values)


def shared_part(flat):
    for bit in range(extra_bits()):
        other = exchanged(flat, 1 << bit)
        mine_first = (lax.axis_index(AXES) >> bit) & 1 == 0
        flat = jnp.where(
            mine_first, jnp.concatenate([flat, other]), jnp.concatenate([other, flat])
        )
    return flat


def own_part(flat):
    for bit in reversed(range(extra_bits())):
        halves = jnp.split(flat, 2)
        mine_first = (lax.axis_index(AXES) >> bit) & 1 == 0
        keep = jnp.where(mine_first, halves[0], halves[1])
        send = jnp.where(mine_first, halves[1], halves[0]).astype(BF16)
        flat = keep + exchanged(send, 1 << bit).astype(F32)
    return flat


def pieces_z(piece):
    return [piece] + [exchanged_part(piece, k << Z_BITS[0]) for k in range(1, 4)]


def gather_step(piece, bit):
    return jnp.concatenate([piece, exchanged_part(piece, 1 << bit)], axis=0)


def reduce_step(state, bit):
    keep, send = state
    total = keep.astype(F32) + exchanged_part(send, 1 << bit).astype(F32)
    half = total.shape[0] // 2
    return total[:half].astype(BF16), total[half:].astype(BF16)


def reduce_total(state, bit):
    keep, send = state
    return keep.astype(F32) + exchanged_part(send, 1 << bit).astype(F32)


def reduce_z(total, steps, result=None):
    result = total[:MAIN] if result is None else result
    for k in steps:
        piece = total[k * MAIN : (k + 1) * MAIN].astype(BF16)
        result = result + exchanged_part(piece, k << Z_BITS[0]).astype(F32)
    return result


def permutation(slots, me):
    rows = D // PARTS
    first = (jnp.asarray(slots) ^ me)[:, None] * rows
    inner = jnp.arange(MAIN, dtype=jnp.int32)[None, :]
    target = jnp.concatenate([(first + inner).reshape(-1), (first + MAIN + inner % 4).reshape(-1)])
    return (jnp.arange(D, dtype=jnp.int32)[:, None] == target[None, :]).astype(BF16)


def local(
    tokens, positions, cotangent, w_query, w_key, w_value, w_out, w_gate, w_up, w_down, gains
):
    me = lax.axis_index(AXES) >> extra_bits()
    block_index = lax.axis_index("seq")
    where = jnp.stack([me, block_index]).astype(jnp.int32)
    parts = [
        shared_part(w).reshape(-1, LANES)
        for w in (w_query, w_key, w_value, w_out, w_gate, w_up, w_down)
    ]
    gain_part = shared_part(gains)
    gain_each = gain_part.shape[0]
    gain_block = jnp.pad(gain_part[None, :], ((0, MAIN - 1), (0, LANES - gain_each)))
    attn, ffn = call(
        pack_kernel,
        [((MAIN, ATTN_A + ATTN_B), BF16), ((MAIN, 2 * FFN_A), BF16)],
        parts + [gain_block],
        [((320, LANES), F32), ((MAIN, FF // 4), F32)],
    )
    attn_z, ffn = together(jnp.concatenate(pieces_z(attn), axis=0), ffn)
    ffn_pieces = [ffn, exchanged_part(ffn, 1 << Z_BITS[0])]
    attn_a, attn_b, ffn_pieces = together(
        gather_step(attn_z[:, :ATTN_A], ORDER_A[0]),
        gather_step(attn_z[:, ATTN_A:], ORDER_B[0]),
        ffn_pieces,
    )
    ffn_pieces.append(exchanged_part(ffn_pieces[0], 2 << Z_BITS[0]))
    attn_a, attn_b, ffn_pieces = together(
        gather_step(attn_a, ORDER_A[1]), gather_step(attn_b, ORDER_B[1]), ffn_pieces
    )
    other_a = exchanged_part(attn_a, 1 << CORE)
    other_b = exchanged_part(attn_b, 1 << CORE)
    ffn_pieces.append(exchanged_part(ffn_pieces[0], 3 << Z_BITS[0]))

    perm_a = permutation(SLOTS_A, me)
    perm_b = permutation(SLOTS_B, me)
    row = jnp.arange(DEPTH, dtype=jnp.int32)

    def picked(slots):
        owner = jnp.repeat(jnp.asarray(slots), MAIN) ^ me
        same = owner[None, :] == jnp.arange(PARTS, dtype=jnp.int32)[:, None]
        return same & (row % MAIN == 0)[None, :]

    gain_pick = picked(SLOTS_A).astype(BF16)
    gain_at = QW + QW // 4
    gain_all = (
        dot(gain_pick[:, :HALF], attn_a[:, gain_at:])
        + dot(gain_pick[:, HALF:], other_a[:, gain_at:])
    )[:, :gain_each].reshape(-1)
    gain_d = gain_all[: 4 * D].reshape(4, D)
    gain_h = gain_all[4 * D :].reshape(2, HD)

    freq_table = 10000.0 ** (-2.0 * jnp.arange(HD // 2, dtype=F32) / HD)
    angle_rows = positions.astype(F32)[:, None] * freq_table[None, :]
    cos_rows = jnp.cos(angle_rows)
    sin_rows = jnp.sin(angle_rows)
    places = positions[:, None]

    rows = (BLK, 2 * DEPTH)
    query_low, kv_low, query_raw, key_raw, one_a, one_b = call(
        qkv_kernel,
        [
            ((BLK, QW), BF16),
            ((BLK, 2 * HD), BF16),
            ((BLK, QW), F32),
            ((BLK, HD), F32),
            (rows, BF16),
            (rows, BF16),
        ],
        [tokens, gain_d, gain_h, perm_a, perm_b, attn_a, other_a, attn_b, other_b]
        + [cos_rows, sin_rows],
        flops=30e9,
    )
    query_low, kv_low, ffn_z = together(query_low, kv_low, jnp.concatenate(ffn_pieces, axis=0))
    earlier = [passed_along(kv_low, "seq", back_step) for back_step in range(BACK, 0, -1)]
    kv_all, ffn_a, ffn_b = together(
        jnp.concatenate(earlier + [kv_low], axis=0),
        gather_step(ffn_z[:, :FFN_A], ORDER_A[0]),
        gather_step(ffn_z[:, FFN_A:], ORDER_B[0]),
    )
    heads_out, log_total, attn_proj, middle, two_a, two_b, out_w = call(
        attend_kernel,
        [
            ((BLK, QW), BF16),
            ((BLK, HEADS * LANES), F32),
            ((BLK, D), F32),
            ((BLK, D), F32),
            (rows, BF16),
            (rows, BF16),
            ((QW, D), BF16),
        ],
        [where, tokens, places, gain_d, perm_a, perm_b, attn_b, other_b, query_low, kv_all],
        scalars=1,
        flops=30e9,
    )
    middle, two_a, two_b, ffn_a, ffn_b = together(
        middle,
        two_a,
        two_b,
        gather_step(ffn_a, ORDER_A[1]),
        gather_step(ffn_b, ORDER_B[1]),
    )
    ffn_other_a = exchanged_part(ffn_a, 1 << CORE)
    ffn_other_b = exchanged_part(ffn_b, 1 << CORE)
    packed = ((HALF, FFN_A), BF16)
    layer_out, keep_a, send_a, keep_b, send_b, mid_grad, ffn_gg = call(
        ffn_kernel,
        [((BLK, D), BF16), packed, packed, packed, packed, ((BLK, D), F32), ((2, D), F32)],
        [where, middle, cotangent, gain_d, perm_a, perm_b, two_a, two_b]
        + [ffn_a, ffn_other_a, ffn_b, ffn_other_b],
        [
            ((FF, D), BF16),
            ((FF, D), BF16),
            ((BLK, FF), F32),
            ((BLK, FF), F32),
            ((BLK, FF), BF16),
            ((BLK, FF), BF16),
            ((BLK, FF), BF16),
            (rows, F32),
            (rows, F32),
        ],
        scalars=1,
        flops=1e6,
    )
    ffn_a = reduce_step((keep_a, send_a), CORE)
    ffn_b = reduce_step((keep_b, send_b), CORE)
    mid_grad_then, ffn_a, ffn_b = together(mid_grad, ffn_a, ffn_b)
    sixteen = ((HALF, QW + QW // 4), BF16)
    (
        kv_earlier,
        kv_own,
        query_keep,
        query_send,
        out_keep,
        out_send,
        back_a,
        attn_out_gg,
        query_gg,
    ) = call(
        attend_back_kernel,
        [
            ((BACK * BLK, 2 * HD), BF16),
            ((BLK, 2 * HD), F32),
            sixteen,
            sixteen,
            sixteen,
            sixteen,
            (rows, F32),
            ((1, D), F32),
            ((1, HD), F32),
        ],
        [where, mid_grad_then, attn_proj, places, gain_d, gain_h, out_w, heads_out, query_low]
        + [kv_all, log_total, query_raw, cos_rows, sin_rows, one_a, attn_a, other_a],
        [((QW, D), BF16), ((SPAN, 2 * HD), F32), ((BLK, QW), BF16)],
        scalars=1,
        flops=1e6,
    )
    ffn_a = reduce_step(ffn_a, ORDER_A[1])
    ffn_b = reduce_step(ffn_b, ORDER_B[1])
    kv_earlier, query_send, out_send, ffn_a, ffn_b = together(
        kv_earlier, query_send, out_send, ffn_a, ffn_b
    )
    came = [
        passed_along(kv_earlier[(BACK - step) * BLK : (BACK - step + 1) * BLK], "seq", -step)
        for step in range(1, BACK + 1)
    ]
    query_state = reduce_step((query_keep, query_send), CORE)
    out_state = reduce_step((out_keep, out_send), CORE)
    ffn_a = reduce_total(ffn_a, ORDER_A[0])
    ffn_b = reduce_total(ffn_b, ORDER_B[0])
    came, query_state, out_state, ffn_a, ffn_b = together(
        came, query_state, out_state, ffn_a, ffn_b
    )
    input_grad, kv_keep, kv_send, attn_in_gg, key_gg = call(
        input_kernel,
        [
            ((BLK, D), F32),
            ((HALF, 2 * HD + LANES), BF16),
            ((HALF, 2 * HD + LANES), BF16),
            ((1, D), F32),
            ((1, HD), F32),
        ],
        [tokens, mid_grad, gain_d, gain_h, perm_a, perm_b, one_b, attn_b, other_b]
        + [kv_own]
        + came
        + [key_raw, cos_rows, sin_rows, back_a],
        flops=1e6,
    )
    query_state = reduce_step(query_state, ORDER_A[1])
    out_state = reduce_step(out_state, ORDER_B[1])
    ffn = [reduce_z(total, (1, 2)) for total in (ffn_a, ffn_b)]
    kv_keep, kv_send, query_state, out_state, ffn = together(
        kv_keep, kv_send, query_state, out_state, ffn
    )
    gains_grad = jnp.concatenate(
        [attn_in_gg[0], attn_out_gg[0], ffn_gg[1], ffn_gg[0], query_gg[0], key_gg[0]]
    )
    gain_rows = lax.dot_general(
        picked(SLOTS_B).astype(F32),
        jnp.pad(gains_grad.reshape(PARTS, gain_each), ((0, 0), (0, LANES - gain_each))),
        (((0,), (0,)), ((), ())),
        precision=lax.Precision.HIGHEST,
        preferred_element_type=F32,
    ).astype(BF16)
    kv_state = (
        jnp.concatenate([kv_keep, gain_rows[:HALF]], axis=1),
        jnp.concatenate([kv_send, gain_rows[HALF:]], axis=1),
    )
    kv_state = reduce_step(reduce_step(kv_state, CORE), ORDER_B[1])
    query_total = reduce_total(query_state, ORDER_A[0])
    out_total = reduce_total(out_state, ORDER_B[0])
    ffn = [reduce_z(total, (3,), result) for total, result in zip((ffn_a, ffn_b), ffn)]
    kv_state, query_total, out_total, ffn = together(kv_state, query_total, out_total, ffn)
    kv_total = reduce_total(kv_state, ORDER_B[0])
    query_sum = reduce_z(query_total, (1, 2, 3))
    out_sum = reduce_z(out_total, (1, 2, 3))
    kv_total, query_sum, out_sum = together(kv_total, query_sum, out_sum)
    kv_sum = reduce_z(kv_total, (1, 2, 3))
    flat = [((160, LANES), F32), ((40, LANES), F32), ((320, LANES), F32)]
    grad_gate, grad_up, grad_down = call(unpack_ffn_kernel, [flat[2]] * 3, ffn)
    grad_query, grad_key, grad_value, grad_out = call(
        unpack_attn_kernel, [flat[0], flat[1], flat[1], flat[0]], [query_sum, out_sum, kv_sum]
    )
    return (
        layer_out,
        input_grad,
        *(
            own_part(grad.reshape(-1))
            for grad in (
                grad_query,
                grad_key,
                grad_value,
                grad_out,
                grad_gate,
                grad_up,
                grad_down,
                kv_sum[0, 2 * HD + LANES : 2 * HD + LANES + gain_each],
            )
        ),
    )


def solution(mesh):
    rows = P(AXES, None)
    flat = P(AXES)
    return jax.shard_map(
        local,
        mesh=mesh,
        in_specs=(rows, flat, rows) + (flat,) * 8,
        out_specs=(rows, rows) + (flat,) * 8,
        check_vma=False,
    )
```

profile of v0, /device:TPU:0, one launch (start us, length us, event | category | flops | bytes accessed | tf_op | source)
XLA Modules:
  0.0 259.1 jit_solution(2976196245042237113)
XLA Ops:
  0.6 1.3 pad.8.gains
  1.9 1.9 shard_map.204
  3.8 3.0 %collective-permute-start = (bf16[16,3328]{1,0:T(8,128)(2,1)}, bf16[16,3328]{1,0:T(8,128)(2,1)S(1)}, u32[]{:S(2)}, u32[]{:S(2)}) collective-permute-start(bf16[16,3328]{1,0:T(8,128)(2,1)} %get-tuple-element.112), channel_id=1, source_target_pairs={{0,2},{1,3},{2,0},{3,1},{4,6},{5,7},{6,4},{7,5},{8,10},{9,11},{10,... | collective-permute-start | bytes 319496 | tf_op jit(solution)/shard_map/ppermute | solution.py:57
  6.9 2.6 collective-permute-start.1
  10.5 1.5 fusion.perm_a
  12.2 5.9 %collective-permute-done.1 = bf16[16,3328]{1,0:T(8,128)(2,1)S(1)} collective-permute-done((bf16[16,3328]{1,0:T(8,128)(2,1)}, bf16[16,3328]{1,0:T(8,128)(2,1)S(1)}, u32[]{:S(2)}, u32[]{:S(2)}) %collective-permute-start.1) | collective-permute-done | bytes 106528 | tf_op jit(solution)/shard_map/ppermute | solution.py:57
  19.1 1.6 collective-permute-start.4
  20.7 1.5 collective-permute-start.3
  22.2 1.5 fusion.1.perm_b
  23.7 1.7 collective-permute-start.5
  26.3 3.8 %collective-permute-done.5 = bf16[16,7680]{1,0:T(8,128)(2,1)S(1)} collective-permute-done((bf16[16,7680]{1,0:T(8,128)(2,1)}, bf16[16,7680]{1,0:T(8,128)(2,1)S(1)}, u32[]{:S(2)}, u32[]{:S(2)}) %collective-permute-start.5) | collective-permute-done | bytes 245792 | tf_op jit(solution)/shard_map/ppermute | solution.py:57
  31.5 1.2 multiply_sine_fusion
  32.8 2.7 %collective-permute-start.8 = (bf16[16,7680]{1,0:T(8,128)(2,1)}, bf16[16,7680]{1,0:T(8,128)(2,1)S(1)}, u32[]{:S(2)}, u32[]{:S(2)}) collective-permute-start(bf16[16,7680]{1,0:T(8,128)(2,1)} %get-tuple-element.124), channel_id=1, source_target_pairs={{0,4},{1,5},{2,6},{3,7},{4,0},{5,1},{6,2},{7,3},{8,12},{9,13},{10,... | collective-permute-start | bytes 737288 | tf_op jit(solution)/shard_map/ppermute | solution.py:57
  35.5 2.1 collective-permute-done.6
  37.6 3.2 %collective-permute-done.7 = bf16[128,1920]{1,0:T(8,128)(2,1)S(1)} collective-permute-done((bf16[128,1920]{1,0:T(8,128)(2,1)S(1)}, bf16[128,1920]{1,0:T(8,128)(2,1)S(1)}, u32[]{:S(2)}, u32[]{:S(2)}) %collective-permute-start.7) | collective-permute-done | bytes 491552 | tf_op jit(solution)/shard_map/ppermute | solution.py:57
  40.9 3.1 %collective-permute-done.8 = bf16[16,7680]{1,0:T(8,128)(2,1)S(1)} collective-permute-done((bf16[16,7680]{1,0:T(8,128)(2,1)}, bf16[16,7680]{1,0:T(8,128)(2,1)S(1)}, u32[]{:S(2)}, u32[]{:S(2)}) %collective-permute-start.8) | collective-permute-done | bytes 245792 | tf_op jit(solution)/shard_map/ppermute | solution.py:57
  44.0 2.7 %collective-permute-start.11 = (bf16[16,7680]{1,0:T(8,128)(2,1)}, bf16[16,7680]{1,0:T(8,128)(2,1)S(1)}, u32[]{:S(2)}, u32[]{:S(2)}) collective-permute-start(bf16[16,7680]{1,0:T(8,128)(2,1)} %get-tuple-element.124), channel_id=1, source_target_pairs={{0,6},{1,7},{2,4},{3,5},{4,2},{5,3},{6,0},{7,1},{8,14},{9,15},{10,... | collective-permute-start | bytes 737288 | tf_op jit(solution)/shard_map/ppermute | solution.py:57
  47.4 5.2 %collective-permute-done.11 = bf16[16,7680]{1,0:T(8,128)(2,1)S(1)} collective-permute-done((bf16[16,7680]{1,0:T(8,128)(2,1)}, bf16[16,7680]{1,0:T(8,128)(2,1)S(1)}, u32[]{:S(2)}, u32[]{:S(2)}) %collective-permute-start.11) | collective-permute-done | bytes 245792 | tf_op jit(solution)/shard_map/ppermute | solution.py:57
  56.1 6.2 %shard_map.205 = (bf16[256,1024]{1,0:T(8,128)(2,1)}, bf16[256,512]{1,0:T(8,128)(2,1)}, f32[256,1024]{1,0:T(8,128)}, f32[256,256]{1,0:T(8,128)}, bf16[256,1024]{1,0:T(8,128)(2,1)}, /*index=5*/bf16[256,1024]{1,0:T(8,128)(2,1)}) custom-call(bf16[256,640]{1,0:T(8,128)(2,1)} %tokens.5, f32[4,640]{1,0:T(4,128)} %reshape.155.gain_d, f32[2,256]{1,0:T(2,128)} %slice.277.gain_h, ...), custom_call_target="tpu_custom_call" | custom-call | flops 30000001024 | tf_op jit(solution)/shard_map/pallas_call | solution.py:495
  63.3 5.0 %collective-permute-start.12 = (bf16[256,512]{1,0:T(8,128)(2,1)S(1)}, bf16[256,512]{1,0:T(8,128)(2,1)S(1)}, u32[]{:S(2)}, u32[]{:S(2)}) collective-permute-start(bf16[256,512]{1,0:T(8,128)(2,1)S(1)} %copy-done.15), channel_id=1, source_target_pairs={{0,2},{1,3},{2,4},{3,5},{4,6},{5,7},{8,10},{9,11},{10,12},{11,13},... | collective-permute-start | bytes 786440 | tf_op jit(solution)/shard_map/ppermute | solution.py:67
  68.3 5.2 %collective-permute-start.13 = (bf16[256,512]{1,0:T(8,128)(2,1)S(1)}, bf16[256,512]{1,0:T(8,128)(2,1)S(1)}, u32[]{:S(2)}, u32[]{:S(2)}) collective-permute-start(bf16[256,512]{1,0:T(8,128)(2,1)S(1)} %copy-done.15), channel_id=1, source_target_pairs={{0,1},{1,2},{2,3},{3,4},{4,5},{5,6},{6,7},{8,9},{9,10},{10,11},{11... | collective-permute-start | bytes 786440 | tf_op jit(solution)/shard_map/ppermute | solution.py:67
  75.0 4.9 %collective-permute-done.13 = bf16[256,512]{1,0:T(8,128)(2,1)S(1)} collective-permute-done((bf16[256,512]{1,0:T(8,128)(2,1)S(1)}, bf16[256,512]{1,0:T(8,128)(2,1)S(1)}, u32[]{:S(2)}, u32[]{:S(2)}) %collective-permute-start.13) | collective-permute-done | bytes 262176 | tf_op jit(solution)/shard_map/ppermute | solution.py:67
  80.9 6.8 %collective-permute-done.14 = bf16[64,3840]{1,0:T(8,128)(2,1)S(1)} collective-permute-done((bf16[64,3840]{1,0:T(8,128)(2,1)S(1)}, bf16[64,3840]{1,0:T(8,128)(2,1)S(1)}, u32[]{:S(2)}, u32[]{:S(2)}) %collective-permute-start.14) | collective-permute-done | bytes 491552 | tf_op jit(solution)/shard_map/ppermute | solution.py:57
  87.7 2.5 collective-permute-start.17
  91.1 7.6 %shard_map.206 = (bf16[256,1024]{1,0:T(8,128)(2,1)}, f32[256,512]{1,0:T(8,128)}, f32[256,640]{1,0:T(8,128)}, f32[256,640]{1,0:T(8,128)}, bf16[256,1024]{1,0:T(8,...) custom-call(s32[2]{0:T(128)} %pad_add_fusion.2.where, bf16[256,640]{1,0:T(8,128)(2,1)} %tokens.5, ...), custom_call_target="tpu_custom_call" | custom-call | flops 30000001024 | tf_op jit(solution)/shard_map/pallas_call | solution.py:495
  98.7 7.5 %collective-permute-done.17 = bf16[128,3840]{1,0:T(8,128)(2,1)S(1)} collective-permute-done((bf16[128,3840]{1,0:T(8,128)(2,1)S(1)}, bf16[128,3840]{1,0:T(8,128)(2,1)S(1)}, u32[]{:S(2)}, u32[]{:S(2)}) %collective-permute-start.17) | collective-permute-done | bytes 983072 | tf_op jit(solution)/shard_map/ppermute | solution.py:57
  106.5 1.1 copy-done
  107.6 2.9 %collective-permute-done.18.other_a = bf16[256,3840]{1,0:T(8,128)(2,1)S(1)} collective-permute-done((bf16[256,3840]{1,0:T(8,128)(2,1)S(1)}, bf16[256,3840]{1,0:T(8,128)(2,1)S(1)}, u32[]{:S(2)}, u32[]{:S(2)}) %collective-permute-start.18) | collective-permute-done | bytes 1966112 | tf_op jit(solution)/shard_map/ppermute | solution.py:57
  110.5 2.8 %collective-permute-done.19.other_b = bf16[256,3840]{1,0:T(8,128)(2,1)S(1)} collective-permute-done((bf16[256,3840]{1,0:T(8,128)(2,1)S(1)}, bf16[256,3840]{1,0:T(8,128)(2,1)S(1)}, u32[]{:S(2)}, u32[]{:S(2)}) %collective-permute-start.19) | collective-permute-done | bytes 1966112 | tf_op jit(solution)/shard_map/ppermute | solution.py:57
  113.3 1.3 copy-done.6
  114.7 26.2 %shard_map.207 = (bf16[256,640]{1,0:T(8,128)(2,1)}, bf16[256,3840]{1,0:T(8,128)(2,1)}, bf16[256,3840]{1,0:T(8,128)(2,1)}, bf16[256,3840]{1,0:T(8,128)(2,1)}, bf1...) custom-call(s32[2]{0:T(128)} %pad_add_fusion.2.where, f32[256,640]{1,0:T(8,128)} %get-tuple-element.136.middle, ...), custom_call_target="tpu_custom_call" | custom-call | flops 1000000 | tf_op jit(solution)/shard_map/pallas_call | solution.py:495
  141.3 3.7 %collective-permute-done.21 = bf16[256,3840]{1,0:T(8,128)(2,1)S(1)} collective-permute-done((bf16[256,3840]{1,0:T(8,128)(2,1)}, bf16[256,3840]{1,0:T(8,128)(2,1)S(1)}, u32[]{:S(2)}, u32[]{:S(2)}) %collective-permute-start.21) | collective-permute-done | bytes 1966112 | tf_op jit(solution)/shard_map/ppermute | solution.py:57
  145.0 2.0 add_convert_fusion
  149.2 2.6 collective-permute-start.23
  151.7 1.1 collective-permute-start.22
  152.8 12.3 %shard_map.208 = (bf16[512,512]{1,0:T(8,128)(2,1)}, f32[256,512]{1,0:T(8,128)}, bf16[256,1280]{1,0:T(8,128)(2,1)}, bf16[256,1280]{1,0:T(8,128)(2,1)}, bf16[256,1...) custom-call(s32[2]{0:T(128)} %pad_add_fusion.2.where, ...), custom_call_target="tpu_custom_call" | custom-call | flops 1000000 | tf_op jit(solution)/shard_map/pallas_call | solution.py:495
  165.1 8.7 %collective-permute-done.23 = bf16[128,3840]{1,0:T(8,128)(2,1)S(1)} collective-permute-done((bf16[128,3840]{1,0:T(8,128)(2,1)S(1)}, bf16[128,3840]{1,0:T(8,128)(2,1)S(1)}, u32[]{:S(2)}, u32[]{:S(2)}) %collective-permute-start.23) | collective-permute-done | bytes 983072 | tf_op jit(solution)/shard_map/ppermute | solution.py:57
  174.1 1.1 collective-permute-done.22
  175.5 1.2 collective-permute-start.29
  178.2 1.3 collective-permute-start.24
  179.5 8.3 %collective-permute-done.29 = bf16[64,3840]{1,0:T(8,128)(2,1)S(1)} collective-permute-done((bf16[64,3840]{1,0:T(8,128)(2,1)S(1)}, bf16[64,3840]{1,0:T(8,128)(2,1)S(1)}, u32[]{:S(2)}, u32[]{:S(2)}) %collective-permute-start.29) | collective-permute-done | bytes 491552 | tf_op jit(solution)/shard_map/ppermute | solution.py:57
  187.7 1.7 collective-permute-start.25
  189.5 3.4 %collective-permute-done.28 = bf16[64,3840]{1,0:T(8,128)(2,1)S(1)} collective-permute-done((bf16[64,3840]{1,0:T(8,128)(2,1)S(1)}, bf16[64,3840]{1,0:T(8,128)(2,1)S(1)}, u32[]{:S(2)}, u32[]{:S(2)}) %collective-permute-start.28) | collective-permute-done | bytes 491552 | tf_op jit(solution)/shard_map/ppermute | solution.py:57
  194.4 1.9 collective-permute-done.25.came_two
  197.2 1.8 collective-permute-start.34
  200.8 2.1 collective-permute-start.33
  202.9 1.3 collective-permute-start.31
  204.2 7.5 %shard_map.209 = (f32[256,640]{1,0:T(8,128)}, bf16[256,640]{1,0:T(8,128)(2,1)}, bf16[256,640]{1,0:T(8,128)(2,1)}, f32[1,640]{1,0:T(1,128)}, f32[1,256]{1,0:T(1,128)}) custom-call(bf16[256,640]{1,0:T(8,128)(2,1)} %tokens.5, f32[256,640]{1,0:T(8,128)} %get-tuple-element.148.mid_grad, f32[4,640]{1,0:T(4,128)} %reshape.155.gain_d, f32[2,256]{1,0:T(2,128)} %slice.277.gain_h, ...), custom_call_target="tpu_custom_call" | custom-call | flops 1000000 | tf_op jit(solution)/shard_map/pallas_call | solution.py:495
  214.9 1.2 collective-permute-start.30
  216.1 1.2 collective-permute-start.41
  218.3 2.7 %collective-permute-start.40 = (bf16[16,3840]{1,0:T(8,128)(2,1)S(1)}, bf16[16,3840]{1,0:T(8,128)(2,1)S(1)}, u32[]{:S(2)}, u32[]{:S(2)}) collective-permute-start(bf16[16,3840]{1,0:T(8,128)(2,1)S(1)} %get-tuple-element.235), channel_id=1, source_target_pairs={{0,6},{1,7},{2,4},{3,5},{4,2},{5,3},{6,0},{7,1},{8,14},{9,15},{10,... | collective-permute-start | bytes 368648 | tf_op jit(solution)/shard_map/ppermute | solution.py:57
  226.7 1.9 collective-permute-done.39
  229.7 4.9 %collective-permute-done.37 = bf16[128,768]{1,0:T(8,128)(2,1)S(1)} collective-permute-done((bf16[128,768]{1,0:T(8,128)(2,1)S(1)}, bf16[128,768]{1,0:T(8,128)(2,1)S(1)}, u32[]{:S(2)}, u32[]{:S(2)}) %collective-permute-start.37) | collective-permute-done | bytes 196640 | tf_op jit(solution)/shard_map/ppermute | solution.py:57
  234.7 2.5 collective-permute-start.46
  237.1 2.4 collective-permute-start.48
  239.6 1.1 collective-permute-start.43
  241.6 2.4 collective-permute-start.45
  244.1 1.1 collective-permute-start.42
  245.9 1.6 collective-permute-done.45
  249.0 2.3 collective-permute-start.50
  251.3 1.9 collective-permute-start.51
  253.2 1.9 shard_map.211
  255.1 1.8 collective-permute-done.51
  257.5 1.6 shard_map.210
  (198 shorter events, 36.9 us)
Async XLA Ops:
  3.8 8.4 %collective-permute-start = (bf16[16,3328]{1,0:T(8,128)(2,1)}, bf16[16,3328]{1,0:T(8,128)(2,1)S(1)}, u32[]{:S(2)}, u32[]{:S(2)}) collective-permute-start(bf16[16,3328]{1,0:T(8,128)(2,1)} %get-tuple-element.112), channel_id=1, source_target_pairs={{0,2},{1,3},{2,0},{3,1},{4,6},{5,7},{6,4},{7,5},{8,10},{9,11},{10,... | collective-permute-start | bytes 319496 | tf_op jit(solution)/shard_map/ppermute | solution.py:57
  6.9 11.3 %collective-permute-start.1 = (bf16[16,3328]{1,0:T(8,128)(2,1)}, bf16[16,3328]{1,0:T(8,128)(2,1)S(1)}, u32[]{:S(2)}, u32[]{:S(2)}) collective-permute-start(bf16[16,3328]{1,0:T(8,128)(2,1)} %get-tuple-element.112), channel_id=1, source_target_pairs={{0,4},{1,5},{2,6},{3,7},{4,0},{5,1},{6,2},{7,3},{8,12},{9,13},{10,... | collective-permute-start | bytes 319496 | tf_op jit(solution)/shard_map/ppermute | solution.py:57
  9.5 8.7 %collective-permute-start.2 = (bf16[16,3328]{1,0:T(8,128)(2,1)}, bf16[16,3328]{1,0:T(8,128)(2,1)S(1)}, u32[]{:S(2)}, u32[]{:S(2)}) collective-permute-start(bf16[16,3328]{1,0:T(8,128)(2,1)} %get-tuple-element.112), channel_id=1, source_target_pairs={{0,6},{1,7},{2,4},{3,5},{4,2},{5,3},{6,0},{7,1},{8,14},{9,15},{10,... | collective-permute-start | bytes 319496 | tf_op jit(solution)/shard_map/ppermute | solution.py:57
  19.1 12.4 %copy-start.20 = (s32[256]{0:T(256)S(1)}, s32[256]{0:T(256)}, u32[]{:S(2)}) copy-start(s32[256]{0:T(256)} %param.14) | copy-start | bytes 3076
  19.1 7.1 %collective-permute-start.4 = (bf16[64,1920]{1,0:T(8,128)(2,1)S(1)}, bf16[64,1920]{1,0:T(8,128)(2,1)S(1)}, u32[]{:S(2)}, u32[]{:S(2)}) collective-permute-start(bf16[64,1920]{1,0:T(8,128)(2,1)S(1)} %slice.214), channel_id=1, source_target_pairs={{0,16},{1,17},{2,18},{3,19},{4,20},{5,21},{6,22},{7,23},{8,24},{9,... | collective-permute-start | bytes 737288 | tf_op jit(solution)/shard_map/ppermute | solution.py:57
  20.7 5.5 %collective-permute-start.3 = (bf16[64,1408]{1,0:T(8,128)(2,1)S(1)}, bf16[64,1408]{1,0:T(8,128)(2,1)S(1)}, u32[]{:S(2)}, u32[]{:S(2)}) collective-permute-start(bf16[64,1408]{1,0:T(8,128)(2,1)S(1)} %slice.213), channel_id=1, source_target_pairs={{0,1},{1,0},{2,3},{3,2},{4,5},{5,4},{6,7},{7,6},{8,9},{9,8},{10,11... | collective-permute-start | bytes 540680 | tf_op jit(solution)/shard_map/ppermute | solution.py:57
  23.7 6.4 %collective-permute-start.5 = (bf16[16,7680]{1,0:T(8,128)(2,1)}, bf16[16,7680]{1,0:T(8,128)(2,1)S(1)}, u32[]{:S(2)}, u32[]{:S(2)}) collective-permute-start(bf16[16,7680]{1,0:T(8,128)(2,1)} %get-tuple-element.124), channel_id=1, source_target_pairs={{0,2},{1,3},{2,0},{3,1},{4,6},{5,7},{6,4},{7,5},{8,10},{9,11},{10,... | collective-permute-start | bytes 737288 | tf_op jit(solution)/shard_map/ppermute | solution.py:57
  30.1 7.4 %collective-permute-start.6 = (bf16[128,1408]{1,0:T(8,128)(2,1)S(1)}, bf16[128,1408]{1,0:T(8,128)(2,1)S(1)}, u32[]{:S(2)}, u32[]{:S(2)}) collective-permute-start(bf16[128,1408]{1,0:T(8,128)(2,1)S(1)} %pad_maximum_fusion.11), channel_id=1, source_target_pairs={{0,16},{1,17},{2,18},{3,19},{4,20},{5,21},{6,22},{7,23},{8,24},{9,... | collective-permute-start | bytes 1081352 | tf_op jit(solution)/shard_map/ppermute | solution.py:57
  30.8 16.6 %copy-start.22 = (pred[512]{0:T(512)(128)(4,1)}, pred[512]{0:T(512)(128)(4,1)S(1)}, u32[]{:S(2)}) copy-start(pred[512]{0:T(512)(128)(4,1)S(1)} %fusion.14) | copy-start | bytes 1540
  30.8 10.0 %collective-permute-start.7 = (bf16[128,1920]{1,0:T(8,128)(2,1)S(1)}, bf16[128,1920]{1,0:T(8,128)(2,1)S(1)}, u32[]{:S(2)}, u32[]{:S(2)}) collective-permute-start(bf16[128,1920]{1,0:T(8,128)(2,1)S(1)} %pad_maximum_fusion.8), channel_id=1, source_target_pairs={{0,1},{1,0},{2,3},{3,2},{4,5},{5,4},{6,7},{7,6},{8,9},{9,8},{10,11... | collective-permute-start | bytes 1474568 | tf_op jit(solution)/shard_map/ppermute | solution.py:57
  31.5 21.1 %copy-start.17 = (bf16[16,7680]{1,0:T(8,128)(2,1)S(1)}, bf16[16,7680]{1,0:T(8,128)(2,1)}, u32[]{:S(2)}) copy-start(bf16[16,7680]{1,0:T(8,128)(2,1)} %copy-done.16) | copy-start | bytes 737284
  32.8 11.2 %collective-permute-start.8 = (bf16[16,7680]{1,0:T(8,128)(2,1)}, bf16[16,7680]{1,0:T(8,128)(2,1)S(1)}, u32[]{:S(2)}, u32[]{:S(2)}) collective-permute-start(bf16[16,7680]{1,0:T(8,128)(2,1)} %get-tuple-element.124), channel_id=1, source_target_pairs={{0,4},{1,5},{2,6},{3,7},{4,0},{5,1},{6,2},{7,3},{8,12},{9,13},{10,... | collective-permute-start | bytes 737288 | tf_op jit(solution)/shard_map/ppermute | solution.py:57
  37.6 16.0 %copy-start.3 = (bf16[256,1408]{1,0:T(8,128)(2,1)}, bf16[256,1408]{1,0:T(8,128)(2,1)S(1)}, u32[]{:S(2)}) copy-start(bf16[256,1408]{1,0:T(8,128)(2,1)S(1)} %pad_maximum_fusion.7.mine_a) | copy-start | bytes 2162692
  40.9 15.2 %copy-start.2 = (bf16[256,1920]{1,0:T(8,128)(2,1)}, bf16[256,1920]{1,0:T(8,128)(2,1)S(1)}, u32[]{:S(2)}) copy-start(bf16[256,1920]{1,0:T(8,128)(2,1)S(1)} %pad_maximum_fusion.2.mine_b) | copy-start | bytes 2949124
  44.0 8.6 %collective-permute-start.11 = (bf16[16,7680]{1,0:T(8,128)(2,1)}, bf16[16,7680]{1,0:T(8,128)(2,1)S(1)}, u32[]{:S(2)}, u32[]{:S(2)}) collective-permute-start(bf16[16,7680]{1,0:T(8,128)(2,1)} %get-tuple-element.124), channel_id=1, source_target_pairs={{0,6},{1,7},{2,4},{3,5},{4,2},{5,3},{6,0},{7,1},{8,14},{9,15},{10,... | collective-permute-start | bytes 737288 | tf_op jit(solution)/shard_map/ppermute | solution.py:57
  46.7 9.4 %collective-permute-start.10 = (bf16[256,1920]{1,0:T(8,128)(2,1)S(1)}, bf16[256,1920]{1,0:T(8,128)(2,1)}, u32[]{:S(2)}, u32[]{:S(2)}) collective-permute-start(bf16[256,1920]{1,0:T(8,128)(2,1)S(1)} %pad_maximum_fusion.2.mine_b), channel_id=1, source_target_pairs={{0,8},{1,9},{2,10},{3,11},{4,12},{5,13},{6,14},{7,15},{8,0},{9,1},... | collective-permute-start | bytes 2949128 | tf_op jit(solution)/shard_map/ppermute | solution.py:57
  46.8 6.9 %collective-permute-start.9 = (bf16[256,1408]{1,0:T(8,128)(2,1)S(1)}, bf16[256,1408]{1,0:T(8,128)(2,1)S(1)}, u32[]{:S(2)}, u32[]{:S(2)}) collective-permute-start(bf16[256,1408]{1,0:T(8,128)(2,1)S(1)} %pad_maximum_fusion.7.mine_a), channel_id=1, source_target_pairs={{0,8},{1,9},{2,10},{3,11},{4,12},{5,13},{6,14},{7,15},{8,0},{9,1},... | collective-permute-start | bytes 2162696 | tf_op jit(solution)/shard_map/ppermute | solution.py:57
  62.3 18.4 %collective-permute-start.15 = (bf16[64,3840]{1,0:T(8,128)(2,1)S(1)}, bf16[64,3840]{1,0:T(8,128)(2,1)S(1)}, u32[]{:S(2)}, u32[]{:S(2)}) collective-permute-start(bf16[64,3840]{1,0:T(8,128)(2,1)S(1)} %get-tuple-element.224), channel_id=1, source_target_pairs={{0,16},{1,17},{2,18},{3,19},{4,20},{5,21},{6,22},{7,23},{8,24},{9,... | collective-permute-start | bytes 1474568 | tf_op jit(solution)/shard_map/ppermute | solution.py:57
  63.3 11.7 %collective-permute-start.12 = (bf16[256,512]{1,0:T(8,128)(2,1)S(1)}, bf16[256,512]{1,0:T(8,128)(2,1)S(1)}, u32[]{:S(2)}, u32[]{:S(2)}) collective-permute-start(bf16[256,512]{1,0:T(8,128)(2,1)S(1)} %copy-done.15), channel_id=1, source_target_pairs={{0,2},{1,3},{2,4},{3,5},{4,6},{5,7},{8,10},{9,11},{10,12},{11,13},... | collective-permute-start | bytes 786440 | tf_op jit(solution)/shard_map/ppermute | solution.py:67
  68.3 11.6 %collective-permute-start.13 = (bf16[256,512]{1,0:T(8,128)(2,1)S(1)}, bf16[256,512]{1,0:T(8,128)(2,1)S(1)}, u32[]{:S(2)}, u32[]{:S(2)}) collective-permute-start(bf16[256,512]{1,0:T(8,128)(2,1)S(1)} %copy-done.15), channel_id=1, source_target_pairs={{0,1},{1,2},{2,3},{3,4},{4,5},{5,6},{6,7},{8,9},{9,10},{10,11},{11... | collective-permute-start | bytes 786440 | tf_op jit(solution)/shard_map/ppermute | solution.py:67
  75.0 12.7 %collective-permute-start.14 = (bf16[64,3840]{1,0:T(8,128)(2,1)S(1)}, bf16[64,3840]{1,0:T(8,128)(2,1)S(1)}, u32[]{:S(2)}, u32[]{:S(2)}) collective-permute-start(bf16[64,3840]{1,0:T(8,128)(2,1)S(1)} %get-tuple-element.225), channel_id=1, source_target_pairs={{0,1},{1,0},{2,3},{3,2},{4,5},{5,4},{6,7},{7,6},{8,9},{9,8},{10,11... | collective-permute-start | bytes 1474568 | tf_op jit(solution)/shard_map/ppermute | solution.py:57
  87.7 18.4 %collective-permute-start.17 = (bf16[128,3840]{1,0:T(8,128)(2,1)S(1)}, bf16[128,3840]{1,0:T(8,128)(2,1)S(1)}, u32[]{:S(2)}, u32[]{:S(2)}) collective-permute-start(bf16[128,3840]{1,0:T(8,128)(2,1)S(1)} %pad_maximum_fusion.5), channel_id=1, source_target_pairs={{0,1},{1,0},{2,3},{3,2},{4,5},{5,4},{6,7},{7,6},{8,9},{9,8},{10,11... | collective-permute-start | bytes 2949128 | tf_op jit(solution)/shard_map/ppermute | solution.py:57
  90.3 16.0 %collective-permute-start.16 = (bf16[128,3840]{1,0:T(8,128)(2,1)S(1)}, bf16[128,3840]{1,0:T(8,128)(2,1)S(1)}, u32[]{:S(2)}, u32[]{:S(2)}) collective-permute-start(bf16[128,3840]{1,0:T(8,128)(2,1)S(1)} %pad_maximum_fusion.4), channel_id=1, source_target_pairs={{0,16},{1,17},{2,18},{3,19},{4,20},{5,21},{6,22},{7,23},{8,24},{9,... | collective-permute-start | bytes 2949128 | tf_op jit(solution)/shard_map/ppermute | solution.py:57
  106.5 6.9 %copy-start.1 = (bf16[256,3840]{1,0:T(8,128)(2,1)}, bf16[256,3840]{1,0:T(8,128)(2,1)S(1)}, u32[]{:S(2)}) copy-start(bf16[256,3840]{1,0:T(8,128)(2,1)S(1)} %pad_maximum_fusion.mine_a) | copy-start | bytes 5898244
  106.5 4.0 %collective-permute-start.18 = (bf16[256,3840]{1,0:T(8,128)(2,1)S(1)}, bf16[256,3840]{1,0:T(8,128)(2,1)S(1)}, u32[]{:S(2)}, u32[]{:S(2)}) collective-permute-start(bf16[256,3840]{1,0:T(8,128)(2,1)S(1)} %pad_maximum_fusion.mine_a), channel_id=1, source_target_pairs={{0,8},{1,9},{2,10},{3,11},{4,12},{5,13},{6,14},{7,15},{8,0},{9,1},... | collective-permute-start | bytes 5898248 | tf_op jit(solution)/shard_map/ppermute | solution.py:57
  107.6 5.7 %collective-permute-start.19 = (bf16[256,3840]{1,0:T(8,128)(2,1)S(1)}, bf16[256,3840]{1,0:T(8,128)(2,1)S(1)}, u32[]{:S(2)}, u32[]{:S(2)}) collective-permute-start(bf16[256,3840]{1,0:T(8,128)(2,1)S(1)} %pad_maximum_fusion.1.mine_b), channel_id=1, source_target_pairs={{0,8},{1,9},{2,10},{3,11},{4,12},{5,13},{6,14},{7,15},{8,0},{9,1},... | collective-permute-start | bytes 5898248 | tf_op jit(solution)/shard_map/ppermute | solution.py:57
  140.8 4.2 %collective-permute-start.21 = (bf16[256,3840]{1,0:T(8,128)(2,1)}, bf16[256,3840]{1,0:T(8,128)(2,1)S(1)}, u32[]{:S(2)}, u32[]{:S(2)}) collective-permute-start(bf16[256,3840]{1,0:T(8,128)(2,1)} %get-tuple-element.147), channel_id=1, source_target_pairs={{0,8},{1,9},{2,10},{3,11},{4,12},{5,13},{6,14},{7,15},{8,0},{9,1},... | collective-permute-start | bytes 5898248 | tf_op jit(solution)/shard_map/ppermute | solution.py:57
  141.0 6.9 %collective-permute-start.20 = (bf16[256,3840]{1,0:T(8,128)(2,1)}, bf16[256,3840]{1,0:T(8,128)(2,1)S(1)}, u32[]{:S(2)}, u32[]{:S(2)}) collective-permute-start(bf16[256,3840]{1,0:T(8,128)(2,1)} %get-tuple-element.145), channel_id=1, source_target_pairs={{0,8},{1,9},{2,10},{3,11},{4,12},{5,13},{6,14},{7,15},{8,0},{9,1},... | collective-permute-start | bytes 5898248 | tf_op jit(solution)/shard_map/ppermute | solution.py:57
  149.2 24.6 %collective-permute-start.23 = (bf16[128,3840]{1,0:T(8,128)(2,1)S(1)}, bf16[128,3840]{1,0:T(8,128)(2,1)S(1)}, u32[]{:S(2)}, u32[]{:S(2)}) collective-permute-start(bf16[128,3840]{1,0:T(8,128)(2,1)S(1)} %get-tuple-element.162), channel_id=1, source_target_pairs={{0,1},{1,0},{2,3},{3,2},{4,5},{5,4},{6,7},{7,6},{8,9},{9,8},{10,11... | collective-permute-start | bytes 2949128 | tf_op jit(solution)/shard_map/ppermute | solution.py:57
  151.7 23.5 %collective-permute-start.22 = (bf16[128,3840]{1,0:T(8,128)(2,1)S(1)}, bf16[128,3840]{1,0:T(8,128)(2,1)S(1)}, u32[]{:S(2)}, u32[]{:S(2)}) collective-permute-start(bf16[128,3840]{1,0:T(8,128)(2,1)S(1)} %get-tuple-element.160), channel_id=1, source_target_pairs={{0,16},{1,17},{2,18},{3,19},{4,20},{5,21},{6,22},{7,23},{8,24},{9,... | collective-permute-start | bytes 2949128 | tf_op jit(solution)/shard_map/ppermute | solution.py:57
  174.1 4.0 %copy-start.10 = (bf16[512,512]{1,0:T(8,128)(2,1)S(1)}, bf16[512,512]{1,0:T(8,128)(2,1)}, u32[]{:S(2)}) copy-start(bf16[512,512]{1,0:T(8,128)(2,1)} %get-tuple-element.163) | copy-start | bytes 1572868
  175.5 12.2 %collective-permute-start.29 = (bf16[64,3840]{1,0:T(8,128)(2,1)S(1)}, bf16[64,3840]{1,0:T(8,128)(2,1)S(1)}, u32[]{:S(2)}, u32[]{:S(2)}) collective-permute-start(bf16[64,3840]{1,0:T(8,128)(2,1)S(1)} %get-tuple-element.171), channel_id=1, source_target_pairs={{0,16},{1,17},{2,18},{3,19},{4,20},{5,21},{6,22},{7,23},{8,24},{9,... | collective-permute-start | bytes 1474568 | tf_op jit(solution)/shard_map/ppermute | solution.py:57
  176.9 16.0 %collective-permute-start.28 = (bf16[64,3840]{1,0:T(8,128)(2,1)S(1)}, bf16[64,3840]{1,0:T(8,128)(2,1)S(1)}, u32[]{:S(2)}, u32[]{:S(2)}) collective-permute-start(bf16[64,3840]{1,0:T(8,128)(2,1)S(1)} %get-tuple-element.169), channel_id=1, source_target_pairs={{0,1},{1,0},{2,3},{3,2},{4,5},{5,4},{6,7},{7,6},{8,9},{9,8},{10,11... | collective-permute-start | bytes 1474568 | tf_op jit(solution)/shard_map/ppermute | solution.py:57
  177.6 15.4 %collective-permute-start.27 = (bf16[256,1280]{1,0:T(8,128)(2,1)}, bf16[256,1280]{1,0:T(8,128)(2,1)S(1)}, u32[]{:S(2)}, u32[]{:S(2)}) collective-permute-start(bf16[256,1280]{1,0:T(8,128)(2,1)} %get-tuple-element.167), channel_id=1, source_target_pairs={{0,8},{1,9},{2,10},{3,11},{4,12},{5,13},{6,14},{7,15},{8,0},{9,1},... | collective-permute-start | bytes 1966088 | tf_op jit(solution)/shard_map/ppermute | solution.py:57
  177.6 15.6 %collective-permute-start.26 = (bf16[256,1280]{1,0:T(8,128)(2,1)}, bf16[256,1280]{1,0:T(8,128)(2,1)S(1)}, u32[]{:S(2)}, u32[]{:S(2)}) collective-permute-start(bf16[256,1280]{1,0:T(8,128)(2,1)} %get-tuple-element.165), channel_id=1, source_target_pairs={{0,8},{1,9},{2,10},{3,11},{4,12},{5,13},{6,14},{7,15},{8,0},{9,1},... | collective-permute-start | bytes 1966088 | tf_op jit(solution)/shard_map/ppermute | solution.py:57
  178.2 16.3 %collective-permute-start.24 = (bf16[256,512]{1,0:T(8,128)(2,1)S(1)}, bf16[256,512]{1,0:T(8,128)(2,1)S(1)}, u32[]{:S(2)}, u32[]{:S(2)}) collective-permute-start(bf16[256,512]{1,0:T(8,128)(2,1)S(1)} %get-tuple-element.231), channel_id=1, source_target_pairs={{1,0},{2,1},{3,2},{4,3},{5,4},{6,5},{7,6},{9,8},{10,9},{11,10},{12... | collective-permute-start | bytes 786440 | tf_op jit(solution)/shard_map/ppermute | solution.py:67
  187.7 5.3 %copy-start.9 = (bf16[256,1280]{1,0:T(8,128)(2,1)S(1)}, bf16[256,1280]{1,0:T(8,128)(2,1)}, u32[]{:S(2)}) copy-start(bf16[256,1280]{1,0:T(8,128)(2,1)} %get-tuple-element.166) | copy-start | bytes 1966084
  187.7 8.6 %collective-permute-start.25 = (bf16[256,512]{1,0:T(8,128)(2,1)S(1)}, bf16[256,512]{1,0:T(8,128)(2,1)S(1)}, u32[]{:S(2)}, u32[]{:S(2)}) collective-permute-start(bf16[256,512]{1,0:T(8,128)(2,1)S(1)} %get-tuple-element.230), channel_id=1, source_target_pairs={{2,0},{3,1},{4,2},{5,3},{6,4},{7,5},{10,8},{11,9},{12,10},{13,11},... | collective-permute-start | bytes 786440 | tf_op jit(solution)/shard_map/ppermute | solution.py:67
  194.4 5.3 %copy-start.13 = (bf16[256,512]{1,0:T(8,128)(2,1)}, bf16[256,512]{1,0:T(8,128)(2,1)S(1)}, u32[]{:S(2)}) copy-start(bf16[256,512]{1,0:T(8,128)(2,1)S(1)} %collective-permute-done.24.came_one) | copy-start | bytes 786436
  196.4 3.4 %copy-start.14 = (bf16[256,512]{1,0:T(8,128)(2,1)}, bf16[256,512]{1,0:T(8,128)(2,1)S(1)}, u32[]{:S(2)}) copy-start(bf16[256,512]{1,0:T(8,128)(2,1)S(1)} %collective-permute-done.25.came_two) | copy-start | bytes 786436
  197.2 17.7 %collective-permute-start.34 = (bf16[16,3840]{1,0:T(8,128)(2,1)}, bf16[16,3840]{1,0:T(8,128)(2,1)}, u32[]{:S(2)}, u32[]{:S(2)}) collective-permute-start(bf16[16,3840]{1,0:T(8,128)(2,1)} %get-tuple-element.234), channel_id=1, source_target_pairs={{0,2},{1,3},{2,0},{3,1},{4,6},{5,7},{6,4},{7,5},{8,10},{9,11},{10,... | collective-permute-start | bytes 368648 | tf_op jit(solution)/shard_map/ppermute | solution.py:57
  199.0 17.1 %collective-permute-start.35 = (bf16[16,3840]{1,0:T(8,128)(2,1)}, bf16[16,3840]{1,0:T(8,128)(2,1)}, u32[]{:S(2)}, u32[]{:S(2)}) collective-permute-start(bf16[16,3840]{1,0:T(8,128)(2,1)} %get-tuple-element.233), channel_id=1, source_target_pairs={{0,4},{1,5},{2,6},{3,7},{4,0},{5,1},{6,2},{7,3},{8,12},{9,13},{10,... | collective-permute-start | bytes 368648 | tf_op jit(solution)/shard_map/ppermute | solution.py:57
  199.7 18.5 %collective-permute-start.32 = (bf16[16,3840]{1,0:T(8,128)(2,1)}, bf16[16,3840]{1,0:T(8,128)(2,1)}, u32[]{:S(2)}, u32[]{:S(2)}) collective-permute-start(bf16[16,3840]{1,0:T(8,128)(2,1)} %get-tuple-element.237), channel_id=1, source_target_pairs={{0,2},{1,3},{2,0},{3,1},{4,6},{5,7},{6,4},{7,5},{8,10},{9,11},{10,... | collective-permute-start | bytes 368648 | tf_op jit(solution)/shard_map/ppermute | solution.py:57
  200.8 20.2 %collective-permute-start.33 = (bf16[16,3840]{1,0:T(8,128)(2,1)}, bf16[16,3840]{1,0:T(8,128)(2,1)}, u32[]{:S(2)}, u32[]{:S(2)}) collective-permute-start(bf16[16,3840]{1,0:T(8,128)(2,1)} %get-tuple-element.236), channel_id=1, source_target_pairs={{0,4},{1,5},{2,6},{3,7},{4,0},{5,1},{6,2},{7,3},{8,12},{9,13},{10,... | collective-permute-start | bytes 368648 | tf_op jit(solution)/shard_map/ppermute | solution.py:57
  202.9 19.1 %collective-permute-start.31 = (bf16[128,1280]{1,0:T(8,128)(2,1)S(1)}, bf16[128,1280]{1,0:T(8,128)(2,1)}, u32[]{:S(2)}, u32[]{:S(2)}) collective-permute-start(bf16[128,1280]{1,0:T(8,128)(2,1)S(1)} %get-tuple-element.182), channel_id=1, source_target_pairs={{0,1},{1,0},{2,3},{3,2},{4,5},{5,4},{6,7},{7,6},{8,9},{9,8},{10,11... | collective-permute-start | bytes 983048 | tf_op jit(solution)/shard_map/ppermute | solution.py:57
  214.9 8.2 %collective-permute-start.30 = (bf16[128,1280]{1,0:T(8,128)(2,1)S(1)}, bf16[128,1280]{1,0:T(8,128)(2,1)S(1)}, u32[]{:S(2)}, u32[]{:S(2)}) collective-permute-start(bf16[128,1280]{1,0:T(8,128)(2,1)S(1)} %get-tuple-element.180), channel_id=1, source_target_pairs={{0,16},{1,17},{2,18},{3,19},{4,20},{5,21},{6,22},{7,23},{8,24},{9,... | collective-permute-start | bytes 983048 | tf_op jit(solution)/shard_map/ppermute | solution.py:57
  216.1 9.2 %collective-permute-start.41 = (bf16[16,3840]{1,0:T(8,128)(2,1)S(1)}, bf16[16,3840]{1,0:T(8,128)(2,1)S(1)}, u32[]{:S(2)}, u32[]{:S(2)}) collective-permute-start(bf16[16,3840]{1,0:T(8,128)(2,1)S(1)} %get-tuple-element.232), channel_id=1, source_target_pairs={{0,6},{1,7},{2,4},{3,5},{4,2},{5,3},{6,0},{7,1},{8,14},{9,15},{10,... | collective-permute-start | bytes 368648 | tf_op jit(solution)/shard_map/ppermute | solution.py:57
  218.2 6.9 %copy-start.12 = (bf16[256,640]{1,0:T(8,128)(2,1)S(1)}, bf16[256,640]{1,0:T(8,128)(2,1)}, u32[]{:S(2)}) copy-start(bf16[256,640]{1,0:T(8,128)(2,1)} %get-tuple-element.191) | copy-start | bytes 983044
  218.3 7.8 %collective-permute-start.40 = (bf16[16,3840]{1,0:T(8,128)(2,1)S(1)}, bf16[16,3840]{1,0:T(8,128)(2,1)S(1)}, u32[]{:S(2)}, u32[]{:S(2)}) collective-permute-start(bf16[16,3840]{1,0:T(8,128)(2,1)S(1)} %get-tuple-element.235), channel_id=1, source_target_pairs={{0,6},{1,7},{2,4},{3,5},{4,2},{5,3},{6,0},{7,1},{8,14},{9,15},{10,... | collective-permute-start | bytes 368648 | tf_op jit(solution)/shard_map/ppermute | solution.py:57
  223.1 5.6 %copy-start.11 = (bf16[256,640]{1,0:T(8,128)(2,1)S(1)}, bf16[256,640]{1,0:T(8,128)(2,1)}, u32[]{:S(2)}) copy-start(bf16[256,640]{1,0:T(8,128)(2,1)} %get-tuple-element.185) | copy-start | bytes 983044
  223.2 5.4 %collective-permute-start.39 = (bf16[64,1280]{1,0:T(8,128)(2,1)S(1)}, bf16[64,1280]{1,0:T(8,128)(2,1)S(1)}, u32[]{:S(2)}, u32[]{:S(2)}) collective-permute-start(bf16[64,1280]{1,0:T(8,128)(2,1)S(1)} %get-tuple-element.195), channel_id=1, source_target_pairs={{0,16},{1,17},{2,18},{3,19},{4,20},{5,21},{6,22},{7,23},{8,24},{9,... | collective-permute-start | bytes 491528 | tf_op jit(solution)/shard_map/ppermute | solution.py:57
  224.2 5.4 %collective-permute-start.38 = (bf16[64,1280]{1,0:T(8,128)(2,1)S(1)}, bf16[64,1280]{1,0:T(8,128)(2,1)S(1)}, u32[]{:S(2)}, u32[]{:S(2)}) collective-permute-start(bf16[64,1280]{1,0:T(8,128)(2,1)S(1)} %get-tuple-element.193), channel_id=1, source_target_pairs={{0,1},{1,0},{2,3},{3,2},{4,5},{5,4},{6,7},{7,6},{8,9},{9,8},{10,11... | collective-permute-start | bytes 491528 | tf_op jit(solution)/shard_map/ppermute | solution.py:57
  225.2 3.5 %collective-permute-start.36 = (bf16[256,768]{1,0:T(8,128)(2,1)S(1)}, bf16[256,768]{1,0:T(8,128)(2,1)S(1)}, u32[]{:S(2)}, u32[]{:S(2)}) collective-permute-start(bf16[256,768]{1,0:T(8,128)(2,1)S(1)} %pad_maximum_fusion.10), channel_id=1, source_target_pairs={{0,8},{1,9},{2,10},{3,11},{4,12},{5,13},{6,14},{7,15},{8,0},{9,1},... | collective-permute-start | bytes 1179656 | tf_op jit(solution)/shard_map/ppermute | solution.py:57
  228.8 5.7 %collective-permute-start.37 = (bf16[128,768]{1,0:T(8,128)(2,1)S(1)}, bf16[128,768]{1,0:T(8,128)(2,1)S(1)}, u32[]{:S(2)}, u32[]{:S(2)}) collective-permute-start(bf16[128,768]{1,0:T(8,128)(2,1)S(1)} %slice.301), channel_id=1, source_target_pairs={{0,1},{1,0},{2,3},{3,2},{4,5},{5,4},{6,7},{7,6},{8,9},{9,8},{10,11... | collective-permute-start | bytes 589832 | tf_op jit(solution)/shard_map/ppermute | solution.py:57
  234.7 7.0 %collective-permute-start.46 = (bf16[16,1280]{1,0:T(8,128)(2,1)S(1)}, bf16[16,1280]{1,0:T(8,128)(2,1)S(1)}, u32[]{:S(2)}, u32[]{:S(2)}) collective-permute-start(bf16[16,1280]{1,0:T(8,128)(2,1)S(1)} %get-tuple-element.244), channel_id=1, source_target_pairs={{0,2},{1,3},{2,0},{3,1},{4,6},{5,7},{6,4},{7,5},{8,10},{9,11},{10,... | collective-permute-start | bytes 122888 | tf_op jit(solution)/shard_map/ppermute | solution.py:57
  237.1 6.9 %collective-permute-start.47 = (bf16[16,1280]{1,0:T(8,128)(2,1)S(1)}, bf16[16,1280]{1,0:T(8,128)(2,1)S(1)}, u32[]{:S(2)}, u32[]{:S(2)}) collective-permute-start(bf16[16,1280]{1,0:T(8,128)(2,1)S(1)} %get-tuple-element.246), channel_id=1, source_target_pairs={{0,4},{1,5},{2,6},{3,7},{4,0},{5,1},{6,2},{7,3},{8,12},{9,13},{10,... | collective-permute-start | bytes 122888 | tf_op jit(solution)/shard_map/ppermute | solution.py:57
  237.1 8.1 %collective-permute-start.48 = (bf16[16,1280]{1,0:T(8,128)(2,1)S(1)}, bf16[16,1280]{1,0:T(8,128)(2,1)S(1)}, u32[]{:S(2)}, u32[]{:S(2)}) collective-permute-start(bf16[16,1280]{1,0:T(8,128)(2,1)S(1)} %get-tuple-element.245), channel_id=1, source_target_pairs={{0,6},{1,7},{2,4},{3,5},{4,2},{5,3},{6,0},{7,1},{8,14},{9,15},{10,... | collective-permute-start | bytes 122888 | tf_op jit(solution)/shard_map/ppermute | solution.py:57
  239.6 6.3 %collective-permute-start.43 = (bf16[16,1280]{1,0:T(8,128)(2,1)S(1)}, bf16[16,1280]{1,0:T(8,128)(2,1)S(1)}, u32[]{:S(2)}, u32[]{:S(2)}) collective-permute-start(bf16[16,1280]{1,0:T(8,128)(2,1)S(1)} %get-tuple-element.247), channel_id=1, source_target_pairs={{0,2},{1,3},{2,0},{3,1},{4,6},{5,7},{6,4},{7,5},{8,10},{9,11},{10,... | collective-permute-start | bytes 122888 | tf_op jit(solution)/shard_map/ppermute | solution.py:57
  240.7 5.2 %collective-permute-start.44 = (bf16[16,1280]{1,0:T(8,128)(2,1)S(1)}, bf16[16,1280]{1,0:T(8,128)(2,1)S(1)}, u32[]{:S(2)}, u32[]{:S(2)}) collective-permute-start(bf16[16,1280]{1,0:T(8,128)(2,1)S(1)} %get-tuple-element.249), channel_id=1, source_target_pairs={{0,4},{1,5},{2,6},{3,7},{4,0},{5,1},{6,2},{7,3},{8,12},{9,13},{10,... | collective-permute-start | bytes 122888 | tf_op jit(solution)/shard_map/ppermute | solution.py:57
  241.6 5.8 %collective-permute-start.45 = (bf16[16,1280]{1,0:T(8,128)(2,1)S(1)}, bf16[16,1280]{1,0:T(8,128)(2,1)S(1)}, u32[]{:S(2)}, u32[]{:S(2)}) collective-permute-start(bf16[16,1280]{1,0:T(8,128)(2,1)S(1)} %get-tuple-element.248), channel_id=1, source_target_pairs={{0,6},{1,7},{2,4},{3,5},{4,2},{5,3},{6,0},{7,1},{8,14},{9,15},{10,... | collective-permute-start | bytes 122888 | tf_op jit(solution)/shard_map/ppermute | solution.py:57
  244.1 4.6 %collective-permute-start.42 = (bf16[64,768]{1,0:T(8,128)(2,1)S(1)}, bf16[64,768]{1,0:T(8,128)(2,1)S(1)}, u32[]{:S(2)}, u32[]{:S(2)}) collective-permute-start(bf16[64,768]{1,0:T(8,128)(2,1)S(1)} %get-tuple-element.199), channel_id=1, source_target_pairs={{0,16},{1,17},{2,18},{3,19},{4,20},{5,21},{6,22},{7,23},{8,24},{9,... | collective-permute-start | bytes 294920 | tf_op jit(solution)/shard_map/ppermute | solution.py:57
  248.7 6.4 %collective-permute-start.49 = (bf16[16,768]{1,0:T(8,128)(2,1)S(1)}, bf16[16,768]{1,0:T(8,128)(2,1)S(1)}, u32[]{:S(2)}, u32[]{:S(2)}) collective-permute-start(bf16[16,768]{1,0:T(8,128)(2,1)S(1)} %get-tuple-element.252), channel_id=1, source_target_pairs={{0,2},{1,3},{2,0},{3,1},{4,6},{5,7},{6,4},{7,5},{8,10},{9,11},{10,... | collective-permute-start | bytes 73736 | tf_op jit(solution)/shard_map/ppermute | solution.py:57
  249.0 6.1 %collective-permute-start.50 = (bf16[16,768]{1,0:T(8,128)(2,1)S(1)}, bf16[16,768]{1,0:T(8,128)(2,1)S(1)}, u32[]{:S(2)}, u32[]{:S(2)}) collective-permute-start(bf16[16,768]{1,0:T(8,128)(2,1)S(1)} %get-tuple-element.254), channel_id=1, source_target_pairs={{0,4},{1,5},{2,6},{3,7},{4,0},{5,1},{6,2},{7,3},{8,12},{9,13},{10,... | collective-permute-start | bytes 73736 | tf_op jit(solution)/shard_map/ppermute | solution.py:57
  251.3 5.6 %collective-permute-start.51 = (bf16[16,768]{1,0:T(8,128)(2,1)S(1)}, bf16[16,768]{1,0:T(8,128)(2,1)S(1)}, u32[]{:S(2)}, u32[]{:S(2)}) collective-permute-start(bf16[16,768]{1,0:T(8,128)(2,1)S(1)} %get-tuple-element.253), channel_id=1, source_target_pairs={{0,6},{1,7},{2,4},{3,5},{4,2},{5,3},{6,0},{7,1},{8,14},{9,15},{10,... | collective-permute-start | bytes 73736 | tf_op jit(solution)/shard_map/ppermute | solution.py:57
  (11 other events, 16.9 us)
where the time goes:
time: 260 us; the launch traced here: 259 us
  waiting for transfers between devices  87.5 us (34%)
  starting transfers between devices  70.5 us (27%)
  Pallas kernels  65.2 us (25%)
  other arithmetic  19.8 us (8%)
  local copies, waits for them, and re-layouts  13.4 us (5%)
    ppermute x48, waiting for transfers between devices, exchanged(): return lax.ppermute(value, AXES, [(i, i ^ mask) for i in range(count)])  80.5 us
    pallas_call x8, Pallas kernels, call(): pl.pallas_call(kernel, out_shape=shapes, in_specs=[pl.BlockSpec(memory_sp...  65.2 us
    ppermute x48, starting transfers between devices, exchanged(): return lax.ppermute(value, AXES, [(i, i ^ mask) for i in range(count)])  57.3 us
    ppermute x4, starting transfers between devices, passed_along(): lax.ppermute(value, axis, [(source, source + steps) for source in range(f...  13.2 us
    ppermute x4, waiting for transfers between devices, passed_along(): lax.ppermute(value, axis, [(source, source + steps) for source in range(f...  6.92 us
    unnamed x51, local copies, waits for them, and re-layouts  5.91 us
  transfers between devices with their start and end apart: 52, of which 25 were waited for; matrix products, arithmetic and copies ran while one was open for 9% of the time, Pallas kernels for 11%

commit v1 on v0

--- a/solution.py
+++ b/solution.py
@@ -175,30 +175,39 @@
             ]
 
 
-def unpack_ffn_kernel(part_a, part_b, gate, up, down):
-    unpack_matrix(part_a, 0, gate)
-    unpack_matrix(part_b, 0, up)
-    unpack_groups(part_a, FF + FF // 4, down, (0, 1))
-    unpack_groups(part_b, FF + FF // 4, down, (2, 3))
-
-
-def unpack_attn_kernel(query_part, out_part, kv_part, query, key, value, out):
-    unpack_matrix(query_part, 0, query)
-    unpack_groups(out_part, 0, out, (0, 1))
+def unpack_ffn_kernel(part, gate, up, down):
+    unpack_matrix(part, 0, gate)
+    unpack_matrix(part, FFN_A, up)
+    unpack_groups(part, FF + FF // 4, down, (0, 1))
+    unpack_groups(part, FFN_A + FF + FF // 4, down, (2, 3))
+
+
+def unpack_attn_kernel(part, query, key, value, out):
+    unpack_matrix(part, 0, query)
+    unpack_groups(part, QW + QW // 4, out, (0, 1))
+    kv_at = QW + QW // 4 + 2 * D
     for place, target in enumerate((key, value)):
         for block in range(2):
-            target[pl.ds(block, MAIN, stride=2), :] = kv_part[
-                :, pl.ds(place * HD + block * LANES, LANES)
+            target[pl.ds(block, MAIN, stride=2), :] = part[
+                :, pl.ds(kv_at + place * HD + block * LANES, LANES)
             ]
             row = 4 * (2 * place + block)
-            target[pl.ds(2 * MAIN + block, 4, stride=2), :] = kv_part[
-                row : row + 4, pl.ds(2 * HD, LANES)
+            target[pl.ds(2 * MAIN + block, 4, stride=2), :] = part[
+                row : row + 4, pl.ds(kv_at + 2 * HD, LANES)
             ]
 
 
+def quarter_mask(shape, dim, quarter):
+    index = lax.broadcasted_iota(jnp.int32, shape, dim)
+    return (index // 4 % 4 == quarter).astype(F32)
+
+
 def quarter_rows(tail_rows, quarter):
-    lane = lax.broadcasted_iota(jnp.int32, tail_rows.shape, 1)
-    return jnp.where(lane // 4 % 4 == quarter, tail_rows, jnp.zeros_like(tail_rows))
+    return tail_rows * quarter_mask((1, DEPTH), 1, quarter).astype(tail_rows.dtype)
+
+
+def quarter_rows_t(tail_rows, quarter):
+    return tail_rows * quarter_mask((DEPTH, 1), 0, quarter).astype(tail_rows.dtype)
 
 
 def packed_product(rows, mine, other, main_at, tail_at, quarter, width):
@@ -228,8 +237,8 @@
     )
 
 
-def packed_grad(rows, incoming, keep, send, main_at):
-    grad = dot(rows, incoming, 0, 0).astype(BF16)
+def packed_grad(rows_t, incoming, keep, send, main_at):
+    grad = dot(rows_t, incoming).astype(BF16)
     main_at = pl.ds(main_at, incoming.shape[1])
     keep[:, main_at] = grad[:HALF]
     send[:, main_at] = grad[HALF:]
@@ -261,10 +270,44 @@
             target[row : row + MAIN, pl.ds(at + place * D, D)] = whole[rows, :]
 
 
+GAIN_SPANS = tuple((i * D, D) for i in range(4)) + ((4 * D, HD), (4 * D + HD, HD))
+GAINS = 4 * D + 2 * HD
+GAIN_EACH = GAINS // PARTS
+
+
+def gain_fold():
+    lane = np.arange(GAINS)[:, None] % GAIN_EACH == np.arange(LANES)[None, :]
+    return jnp.asarray(lane, BF16)
+
+
+def gain_holders(owners, span):
+    entry = span[0] + lax.broadcasted_iota(jnp.int32, (PARTS, span[1]), 1)
+    first = owners[...] * GAIN_EACH
+    return (entry >= first) & (entry < first + GAIN_EACH)
+
+
+def slot_first_rows():
+    row = lax.broadcasted_iota(jnp.int32, (PARTS, DEPTH), 1)
+    return (row == MAIN * lax.broadcasted_iota(jnp.int32, (PARTS, DEPTH), 0)).astype(BF16)
+
+
 def qkv_kernel(
-    tokens, gain_d, gain_h, perm_a, perm_b, mine_a, other_a, mine_b, other_b, cos, sin,
-    query_low, kv_low, query_raw, key_raw, rows_a, rows_b,
+    tokens, owners, fold, perm_a, perm_b, mine_a, other_a, mine_b, other_b, cos, sin,
+    query_low, kv_low, query_raw, key_raw, rows_a, rows_b, gain_d, gain_h,
 ):
+    first_rows = slot_first_rows()
+    gain_at = pl.ds(QW + QW // 4, LANES)
+    gain_rows = (
+        dot(first_rows[:, :HALF], mine_a[:, gain_at])
+        + dot(first_rows[:, HALF:], other_a[:, gain_at])
+    ).astype(BF16)
+    for place, span in enumerate(GAIN_SPANS):
+        spread = dot(gain_rows, fold[span[0] : span[0] + span[1], :], 1, 1)
+        total = row_sum(jnp.where(gain_holders(owners, span), spread, 0.0))
+        if place < 4:
+            gain_d[place : place + 1, :] = total
+        else:
+            gain_h[place - 4 : place - 3, :] = total
     unit, _ = unit_of(tokens[...].astype(F32))
     normed = (unit * gain_d[0:1, :]).astype(BF16)
     rows_a[...] = dot(normed, perm_a[...]).astype(BF16)
@@ -325,89 +368,138 @@
 TANH_SCALE = float(np.sqrt(2.0 / np.pi))
 
 
+def ffn_pieces_in(pieces, weights, sems, spans):
+    copies = [
+        [
+            pltpu.make_async_copy(
+                piece.at[:, pl.ds(*span)],
+                weights[at // 4].at[pl.ds(at % 4 * (DEPTH // 4), DEPTH // 4), pl.ds(*span)],
+                sems.at[8 * place + at],
+            )
+            for at, piece in enumerate(pieces)
+        ]
+        for place, span in enumerate(spans)
+    ]
+    for group in copies:
+        for copy in group:
+            copy.start()
+    return copies
+
+
+def halves(weights):
+    return weights.at[pl.ds(0, HALF)], weights.at[pl.ds(HALF, HALF)]
+
+
 def ffn_kernel(
-    where, middle, cotangent, gain_d, perm_a, perm_b, rows_a, rows_b, mine_a, other_a, mine_b,
-    other_b, layer_out, keep_a, send_a, keep_b, send_b, mid_grad, gain_grad,
-    down_w, down_grad, gate_s, up_s, hidden_s, gate_g, up_g, back_a, back_b,
+    where, middle, cotangent, gain_d, rows_a, rows_b, a_0, a_1, a_2, a_3, b_0, b_1, b_2, b_3,
+    layer_out, keep_a, send_a, keep_b, send_b, gate_g, up_g, gain_grad,
+    weights_a, weights_b, down_w, down_grad, active_s, slope_s, hidden_s, rows_at, rows_bt, sems,
 ):
     me = where[0]
     down_at = FF + FF // 4
+    spans = ((FF, FF // 4), (0, FF // 2), (FF // 2, FF // 2), (down_at, 2 * D))
+    tail_in, first_in, second_in, down_in = ffn_pieces_in(
+        (a_0, a_1, a_2, a_3, b_0, b_1, b_2, b_3), (weights_a, weights_b), sems, spans
+    )
+    rows_at[...] = rows_a[...].T
+    rows_bt[...] = rows_b[...].T
+    mine_a, other_a = halves(weights_a)
+    mine_b, other_b = halves(weights_b)
+
+    def forward(tile):
+        at = pl.multiple_of(tile * TILE, TILE)
+        tail_at = pl.multiple_of(FF + tile % 2 * TILE, TILE)
+        gate = packed_product(rows_a, mine_a, other_a, at, tail_at, tile // 2, TILE)
+        up = packed_product(rows_b, mine_b, other_b, at, tail_at, tile // 2, TILE)
+        cols = pl.ds(at, TILE)
+        square = gate * gate
+        tanh = jnp.tanh(TANH_SCALE * (gate + 0.044715 * gate * square))
+        active = 0.5 * gate * (1.0 + tanh)
+        slope = 0.5 * (1.0 + tanh) + 0.5 * gate * (1.0 - tanh * tanh) * TANH_SCALE * (
+            1.0 + 3.0 * 0.044715 * square
+        )
+        active_s[:, cols] = active
+        slope_s[:, cols] = up * slope
+        hidden_s[:, cols] = (active * up).astype(BF16)
+
+    for copy in tail_in + first_in:
+        copy.wait()
+    pl.loop(0, TILES // 2)(forward)
+    for copy in second_in:
+        copy.wait()
+    pl.loop(TILES // 2, TILES)(forward)
+    for copy in down_in:
+        copy.wait()
     place_groups(down_w, me, SLOTS_A, mine_a, other_a, down_at, (0, 1), 4)
     place_groups(down_w, me, SLOTS_B, mine_b, other_b, down_at, (2, 3), 4)
-
-    def tile_places(tile):
-        at = pl.multiple_of(tile * TILE, TILE)
-        tail_at = pl.multiple_of(FF + tile % 2 * TILE, TILE)
-        return at, tail_at, tile // 2
-
-    @pl.loop(0, TILES)
-    def forward(tile):
-        at, tail_at, quarter = tile_places(tile)
-        gate = packed_product(rows_a, mine_a, other_a, at, tail_at, quarter, TILE)
-        up = packed_product(rows_b, mine_b, other_b, at, tail_at, quarter, TILE)
-        gate_s[:, pl.ds(at, TILE)] = gate
-        up_s[:, pl.ds(at, TILE)] = up
-        tanh = jnp.tanh(TANH_SCALE * (gate + 0.044715 * gate * gate * gate))
-        hidden_s[:, pl.ds(at, TILE)] = (0.5 * gate * (1.0 + tanh) * up).astype(BF16)
-
     proj = dot(hidden_s[...], down_w[...])
-    mid = middle[...]
     unit, inverse = unit_of(proj)
-    layer_out[...] = (mid + unit * gain_d[3:4, :]).astype(BF16)
+    layer_out[...] = (middle[...] + unit * gain_d[3:4, :]).astype(BF16)
     out_grad = cotangent[...].astype(F32)
     gain_grad[0:1, :] = row_sum(out_grad * unit)
     proj_grad = rms_values_grad(out_grad, unit, inverse, gain_d[3:4, :]).astype(BF16)
-    back_a[...] = jnp.zeros_like(back_a)
-    back_b[...] = jnp.zeros_like(back_b)
 
     @pl.loop(0, TILES)
     def backward(tile):
-        at, tail_at, quarter = tile_places(tile)
+        at = pl.multiple_of(tile * TILE, TILE)
         cols = pl.ds(at, TILE)
         hidden_grad = dot(proj_grad, down_w[cols, :], 1, 1)
         down_grad[cols, :] = dot(hidden_s[:, cols], proj_grad, 0, 0).astype(BF16)
-        gate, up = gate_s[:, cols], up_s[:, cols]
-        square = gate * gate
-        tanh = jnp.tanh(TANH_SCALE * (gate + 0.044715 * gate * square))
-        slope = 0.5 * (1.0 + tanh) + 0.5 * gate * (1.0 - tanh * tanh) * TANH_SCALE * (
-            1.0 + 3.0 * 0.044715 * square
-        )
-        gate_grad = (hidden_grad * up * slope).astype(BF16)
-        up_grad = (hidden_grad * (0.5 * gate * (1.0 + tanh))).astype(BF16)
+        gate_grad = (hidden_grad * slope_s[:, cols]).astype(BF16)
+        up_grad = (hidden_grad * active_s[:, cols]).astype(BF16)
         gate_g[:, cols] = gate_grad
         up_g[:, cols] = up_grad
-        back_a[...] += packed_back(gate_grad, mine_a, other_a, at, tail_at, quarter)
-        back_b[...] += packed_back(up_grad, mine_b, other_b, at, tail_at, quarter)
-        packed_grad(rows_a[:, :DEPTH], gate_grad, keep_a, send_a, at)
-        packed_grad(rows_b[:, :DEPTH], up_grad, keep_b, send_b, at)
-
-    for rows, grad_s, keep, send in ((rows_a, gate_g, keep_a, send_a), (rows_b, up_g, keep_b, send_b)):
-
-        @pl.loop(0, 2)
-        def tails(half):
-            total = jnp.zeros((DEPTH, TILE), F32)
-            for quarter in range(4):
-                at = pl.multiple_of(quarter * (FF // 4) + half * TILE, TILE)
-                total += dot(quarter_rows(rows[:, DEPTH:], quarter), grad_s[:, pl.ds(at, TILE)], 0, 0)
-            at = pl.ds(pl.multiple_of(FF + half * TILE, TILE), TILE)
-            keep[:, at] = total[:HALF].astype(BF16)
-            send[:, at] = total[HALF:].astype(BF16)
-
+        packed_grad(rows_at[:DEPTH, :], gate_grad, keep_a, send_a, at)
+        packed_grad(rows_bt[:DEPTH, :], up_grad, keep_b, send_b, at)
+
+    width = FF // 4
+    for rows_t, grad_s, keep, send in (
+        (rows_at, gate_g, keep_a, send_a),
+        (rows_bt, up_g, keep_b, send_b),
+    ):
+        tail_grad = jnp.zeros((DEPTH, width), F32)
+        for quarter in range(4):
+            part = grad_s[:, pl.ds(quarter * width, width)]
+            tail_grad += dot(quarter_rows_t(rows_t[DEPTH:, :], quarter), part)
+        keep[:, pl.ds(FF, width)] = tail_grad[:HALF].astype(BF16)
+        send[:, pl.ds(FF, width)] = tail_grad[HALF:].astype(BF16)
     take_groups(down_grad, me, SLOTS_A, keep_a, send_a, down_at, (0, 1), 4)
     take_groups(down_grad, me, SLOTS_B, keep_b, send_b, down_at, (2, 3), 4)
-    normed_grad = natural_columns(back_a[...], perm_a[...]) + natural_columns(
-        back_b[...], perm_b[...]
-    )
-    unit, inverse = unit_of(mid)
-    gain_grad[1:2, :] = row_sum(normed_grad * unit)
-    mid_grad[...] = out_grad + rms_values_grad(normed_grad, unit, inverse, gain_d[2:3, :])
+
+
+def ffn_back_kernel(
+    middle, cotangent, gain_d, perm_a, perm_b, gate_g, up_g, a_0, a_1, a_2, a_3, b_0, b_1, b_2,
+    b_3, mid_grad, gain_grad, weights_a, weights_b, sems,
+):
+    (copies,) = ffn_pieces_in(
+        (a_0, a_1, a_2, a_3, b_0, b_1, b_2, b_3),
+        (weights_a, weights_b),
+        sems,
+        ((0, FF + FF // 4),),
+    )
+    width = FF // 4
+    normed_grad = jnp.zeros((BLK, D), F32)
+    for at, grad_s, weights, perm in ((0, gate_g, weights_a, perm_a), (4, up_g, weights_b, perm_b)):
+        for copy in copies[at : at + 4]:
+            copy.wait()
+        tail_back = jnp.zeros((BLK, DEPTH), F32)
+        for quarter in range(4):
+            part = grad_s[:, pl.ds(quarter * width, width)]
+            tail_back += quarter_rows(dot(part, weights[:, pl.ds(FF, width)], 1, 1), quarter)
+        back = jnp.concatenate([dot(grad_s[...], weights[:, :FF], 1, 1), tail_back], axis=1)
+        normed_grad += natural_columns(back, perm[...])
+    unit, inverse = unit_of(middle[...])
+    gain_grad[0:1, :] = row_sum(normed_grad * unit)
+    mid_grad[...] = cotangent[...].astype(F32) + rms_values_grad(
+        normed_grad, unit, inverse, gain_d[2:3, :]
+    )
 
 
 def attend_back_kernel(
     where, mid_grad, attn_proj, positions, gain_d, gain_h, out_w, heads_out, query_low, kv_all,
     log_total, query_raw, cos, sin, rows_a, mine_a, other_a,
     kv_earlier, kv_own, query_keep, query_send, out_keep, out_send, back_a, gain_grad_d,
-    gain_grad_h, out_grad_s, kv_grad, query_grad_s,
+    gain_grad_h, out_grad_s, kv_grad, query_grad_s, rows_t,
 ):
     incoming = mid_grad[...]
     unit, inverse = unit_of(attn_proj[...])
@@ -419,6 +511,7 @@
     take_groups(out_grad_s, where[0], SLOTS_B, out_keep, out_send, 0, (0, 1), 2)
     allowed = allowed_pairs(where[1], positions)
     cos_rows, sin_rows = cos[...], sin[...]
+    rows_t[...] = rows_a[...].T
     total_a = jnp.zeros((BLK, 2 * DEPTH), F32)
     gain_total = jnp.zeros((1, HD), F32)
     keys_grad = jnp.zeros((SPAN, HD), F32)
@@ -441,7 +534,7 @@
         raw_grad = rms_values_grad(query_rot, unit, inverse, gain_h[0:1, :]).astype(BF16)
         query_grad_s[:, at] = raw_grad
         total_a += packed_back(raw_grad, mine_a, other_a, head * HD, QW, head)
-        packed_grad(rows_a[:, :DEPTH], raw_grad, query_keep, query_send, head * HD)
+        packed_grad(rows_t[:DEPTH, :], raw_grad, query_keep, query_send, head * HD)
     gain_grad_h[0:1, :] = gain_total
     kv_grad[:, :HD] = keys_grad
     kv_grad[:, HD:] = values_grad
@@ -451,7 +544,7 @@
     tail = jnp.zeros((DEPTH, HD), F32)
     for head in range(HEADS):
         tail += dot(
-            quarter_rows(rows_a[:, DEPTH:], head), query_grad_s[:, pl.ds(head * HD, HD)], 0, 0
+            quarter_rows_t(rows_t[DEPTH:, :], head), query_grad_s[:, pl.ds(head * HD, HD)]
         )
     query_keep[:, pl.ds(QW, HD)] = tail[:HALF].astype(BF16)
     query_send[:, pl.ds(QW, HD)] = tail[HALF:].astype(BF16)
@@ -459,28 +552,39 @@
 
 def input_kernel(
     tokens, mid_grad, gain_d, gain_h, perm_a, perm_b, rows_b, mine_b, other_b, kv_own, came_one,
-    came_two, key_raw, cos, sin, back_a, input_grad, kv_keep, kv_send, gain_grad_d, gain_grad_h,
+    came_two, key_raw, cos, sin, back_a, owners, fold, out_gg, ffn_out_gg, ffn_in_gg, query_gg,
+    input_grad, kv_keep, kv_send, rows_t,
 ):
     total = kv_own[...] + came_one[...].astype(F32) + came_two[...].astype(F32)
     key_rot = rotate(total[:, :HD], cos[...], -sin[...])
     unit, inverse = unit_of(key_raw[...])
-    gain_grad_h[0:1, :] = row_sum(key_rot * unit)
+    key_gg = row_sum(key_rot * unit)
     key_grad = rms_values_grad(key_rot, unit, inverse, gain_h[1:2, :]).astype(BF16)
     raw_grad = jnp.concatenate([key_grad, total[:, HD:].astype(BF16)], axis=1)
+    rows_t[...] = rows_b[...].T
     back_b = jnp.zeros((BLK, 2 * DEPTH), F32)
     tail = jnp.zeros((DEPTH, LANES), F32)
     for c in range(4):
         part = raw_grad[:, c * LANES : (c + 1) * LANES]
         back_b += packed_back(part, mine_b, other_b, c * LANES, 2 * HD, c)
-        tail += dot(quarter_rows(rows_b[:, DEPTH:], c), part, 0, 0)
-    packed_grad(rows_b[:, :DEPTH], raw_grad, kv_keep, kv_send, 0)
+        tail += dot(quarter_rows_t(rows_t[DEPTH:, :], c), part)
+    packed_grad(rows_t[:DEPTH, :], raw_grad, kv_keep, kv_send, 0)
     kv_keep[:, pl.ds(2 * HD, LANES)] = tail[:HALF].astype(BF16)
     kv_send[:, pl.ds(2 * HD, LANES)] = tail[HALF:].astype(BF16)
     normed_grad = natural_columns(back_a[...], perm_a[...]) + natural_columns(
         back_b, perm_b[...]
     )
     unit, inverse = unit_of(tokens[...].astype(F32))
-    gain_grad_d[0:1, :] = row_sum(normed_grad * unit)
+    in_gg = row_sum(normed_grad * unit)
+    gain_grads = (in_gg, out_gg[...], ffn_in_gg[...], ffn_out_gg[...], query_gg[...], key_gg)
+    gain_rows = jnp.zeros((PARTS, LANES), F32)
+    for grad, span in zip(gain_grads, GAIN_SPANS):
+        held = jnp.where(gain_holders(owners, span), grad, 0.0).astype(BF16)
+        gain_rows += dot(held, fold[span[0] : span[0] + span[1], :])
+    gain_rows = dot(slot_first_rows(), gain_rows.astype(BF16), 0, 0).astype(BF16)
+    gain_at = pl.ds(2 * HD + LANES, LANES)
+    kv_keep[:, gain_at] = gain_rows[:HALF]
+    kv_send[:, gain_at] = gain_rows[HALF:]
     input_grad[...] = mid_grad[...] + rms_values_grad(
         normed_grad, unit, inverse, gain_d[0:1, :]
     )
@@ -489,15 +593,20 @@
 VMEM_LIMIT = 56 * 1024 * 1024
 
 
-def call(kernel, outs, args, scratch=(), scalars=0, flops=0):
+def call(kernel, outs, args, scratch=(), scalars=0, left=0, flops=1e6):
     vmem = pl.BlockSpec(memory_space=pltpu.VMEM)
     shapes = [jax.ShapeDtypeStruct(shape, kind) for shape, kind in outs]
+    places = [pl.BlockSpec(memory_space=pltpu.SMEM)] * scalars
+    places += [vmem] * (len(args) - scalars - left) + [pl.BlockSpec(memory_space=pl.ANY)] * left
+    buffers = [pltpu.VMEM(shape, kind) for shape, kind in scratch]
+    if left:
+        buffers.append(pltpu.SemaphoreType.DMA((4 * left,)))
     return pl.pallas_call(
         kernel,
         out_shape=shapes,
-        in_specs=[pl.BlockSpec(memory_space=pltpu.SMEM)] * scalars + [vmem] * (len(args) - scalars),
+        in_specs=places,
         out_specs=[vmem] * len(outs),
-        scratch_shapes=[pltpu.VMEM(shape, kind) for shape, kind in scratch],
+        scratch_shapes=buffers,
         compiler_params=pltpu.CompilerParams(vmem_limit_bytes=VMEM_LIMIT),
         cost_estimate=pl.CostEstimate(flops=int(flops), bytes_accessed=0, transcendentals=0),
     )(*args)
@@ -505,6 +614,10 @@
 
 def together(*values):
     return lax.optimization_barrier(values)
+
+
+def loosely(*values):
+    return values
 
 
 def shared_part(flat):
@@ -531,28 +644,21 @@
     return [piece] + [exchanged_part(piece, k << Z_BITS[0]) for k in range(1, 4)]
 
 
-def gather_step(piece, bit):
-    return jnp.concatenate([piece, exchanged_part(piece, 1 << bit)], axis=0)
-
-
-def reduce_step(state, bit):
-    keep, send = state
-    total = keep.astype(F32) + exchanged_part(send, 1 << bit).astype(F32)
+def stacked(*pieces):
+    return jnp.concatenate(pieces, axis=0)
+
+
+def added(keep, came):
+    return keep.astype(F32) + came.astype(F32)
+
+
+def halved(total):
     half = total.shape[0] // 2
     return total[:half].astype(BF16), total[half:].astype(BF16)
 
 
-def reduce_total(state, bit):
-    keep, send = state
-    return keep.astype(F32) + exchanged_part(send, 1 << bit).astype(F32)
-
-
-def reduce_z(total, steps, result=None):
-    result = total[:MAIN] if result is None else result
-    for k in steps:
-        piece = total[k * MAIN : (k + 1) * MAIN].astype(BF16)
-        result = result + exchanged_part(piece, k << Z_BITS[0]).astype(F32)
-    return result
+def sent_z(total, k):
+    return exchanged_part(total[k * MAIN : (k + 1) * MAIN].astype(BF16), k << Z_BITS[0])
 
 
 def permutation(slots, me):
@@ -582,38 +688,29 @@
         parts + [gain_block],
         [((320, LANES), F32), ((MAIN, FF // 4), F32)],
     )
-    attn_z, ffn = together(jnp.concatenate(pieces_z(attn), axis=0), ffn)
-    ffn_pieces = [ffn, exchanged_part(ffn, 1 << Z_BITS[0])]
-    attn_a, attn_b, ffn_pieces = together(
-        gather_step(attn_z[:, :ATTN_A], ORDER_A[0]),
-        gather_step(attn_z[:, ATTN_A:], ORDER_B[0]),
-        ffn_pieces,
-    )
-    ffn_pieces.append(exchanged_part(ffn_pieces[0], 2 << Z_BITS[0]))
-    attn_a, attn_b, ffn_pieces = together(
-        gather_step(attn_a, ORDER_A[1]), gather_step(attn_b, ORDER_B[1]), ffn_pieces
-    )
+    pieces, ffn = together(pieces_z(attn), ffn)
+    attn_z = stacked(*pieces)
+    attn_a, attn_b = attn_z[:, :ATTN_A], attn_z[:, ATTN_A:]
+    ffn_two = exchanged_part(ffn, 2 << Z_BITS[0])
+    next_a, next_b = exchanged_part(attn_a, 1 << ORDER_A[0]), exchanged_part(attn_b, 1 << ORDER_B[0])
+    next_a, next_b, ffn_two, ffn = loosely(next_a, next_b, ffn_two, ffn)
+    attn_a, attn_b = stacked(attn_a, next_a), stacked(attn_b, next_b)
+    ffn_one = exchanged_part(ffn, 1 << Z_BITS[0])
+    ffn_three = exchanged_part(ffn, 3 << Z_BITS[0])
+    next_a, next_b = exchanged_part(attn_a, 1 << ORDER_A[1]), exchanged_part(attn_b, 1 << ORDER_B[1])
+    next_a, next_b, ffn_one, ffn_three = loosely(next_a, next_b, ffn_one, ffn_three)
+    attn_a, attn_b = stacked(attn_a, next_a), stacked(attn_b, next_b)
     other_a = exchanged_part(attn_a, 1 << CORE)
     other_b = exchanged_part(attn_b, 1 << CORE)
-    ffn_pieces.append(exchanged_part(ffn_pieces[0], 3 << Z_BITS[0]))
+    ffn_z = stacked(ffn, ffn_one, ffn_two, ffn_three)
+    ffn_a, ffn_b = ffn_z[:, :FFN_A], ffn_z[:, FFN_A:]
+    next_a, next_b = exchanged_part(ffn_a, 1 << ORDER_A[0]), exchanged_part(ffn_b, 1 << ORDER_B[0])
 
     perm_a = permutation(SLOTS_A, me)
     perm_b = permutation(SLOTS_B, me)
-    row = jnp.arange(DEPTH, dtype=jnp.int32)
-
-    def picked(slots):
-        owner = jnp.repeat(jnp.asarray(slots), MAIN) ^ me
-        same = owner[None, :] == jnp.arange(PARTS, dtype=jnp.int32)[:, None]
-        return same & (row % MAIN == 0)[None, :]
-
-    gain_pick = picked(SLOTS_A).astype(BF16)
-    gain_at = QW + QW // 4
-    gain_all = (
-        dot(gain_pick[:, :HALF], attn_a[:, gain_at:])
-        + dot(gain_pick[:, HALF:], other_a[:, gain_at:])
-    )[:, :gain_each].reshape(-1)
-    gain_d = gain_all[: 4 * D].reshape(4, D)
-    gain_h = gain_all[4 * D :].reshape(2, HD)
+    owners_a = (jnp.asarray(SLOTS_A) ^ me)[:, None]
+    owners_b = (jnp.asarray(SLOTS_B) ^ me)[:, None]
+    fold = gain_fold()
 
     freq_table = 10000.0 ** (-2.0 * jnp.arange(HD // 2, dtype=F32) / HD)
     angle_rows = positions.astype(F32)[:, None] * freq_table[None, :]
@@ -622,7 +719,7 @@
     places = positions[:, None]
 
     rows = (BLK, 2 * DEPTH)
-    query_low, kv_low, query_raw, key_raw, one_a, one_b = call(
+    query_low, kv_low, query_raw, key_raw, one_a, one_b, gain_d, gain_h = call(
         qkv_kernel,
         [
             ((BLK, QW), BF16),
@@ -631,18 +728,17 @@
             ((BLK, HD), F32),
             (rows, BF16),
             (rows, BF16),
+            ((4, D), F32),
+            ((2, HD), F32),
         ],
-        [tokens, gain_d, gain_h, perm_a, perm_b, attn_a, other_a, attn_b, other_b]
+        [tokens, owners_a, fold, perm_a, perm_b, attn_a, other_a, attn_b, other_b]
         + [cos_rows, sin_rows],
-        flops=30e9,
-    )
-    query_low, kv_low, ffn_z = together(query_low, kv_low, jnp.concatenate(ffn_pieces, axis=0))
+        flops=9e9,
+    )
+    query_low, kv_low, next_a, next_b = loosely(query_low, kv_low, next_a, next_b)
+    ffn_a, ffn_b = stacked(ffn_a, next_a), stacked(ffn_b, next_b)
     earlier = [passed_along(kv_low, "seq", back_step) for back_step in range(BACK, 0, -1)]
-    kv_all, ffn_a, ffn_b = together(
-        jnp.concatenate(earlier + [kv_low], axis=0),
-        gather_step(ffn_z[:, :FFN_A], ORDER_A[0]),
-        gather_step(ffn_z[:, FFN_A:], ORDER_B[0]),
-    )
+    kv_all = jnp.concatenate(earlier + [kv_low], axis=0)
     heads_out, log_total, attn_proj, middle, two_a, two_b, out_w = call(
         attend_kernel,
         [
@@ -656,40 +752,51 @@
         ],
         [where, tokens, places, gain_d, perm_a, perm_b, attn_b, other_b, query_low, kv_all],
         scalars=1,
-        flops=30e9,
-    )
-    middle, two_a, two_b, ffn_a, ffn_b = together(
-        middle,
-        two_a,
-        two_b,
-        gather_step(ffn_a, ORDER_A[1]),
-        gather_step(ffn_b, ORDER_B[1]),
-    )
-    ffn_other_a = exchanged_part(ffn_a, 1 << CORE)
-    ffn_other_b = exchanged_part(ffn_b, 1 << CORE)
+        flops=9e9,
+    )
+    next_a, next_b = exchanged_part(ffn_a, 1 << ORDER_A[1]), exchanged_part(ffn_b, 1 << ORDER_B[1])
+    other_ffn_a, other_ffn_b = exchanged_part(ffn_a, 1 << CORE), exchanged_part(ffn_b, 1 << CORE)
+    middle, two_a, two_b, next_a, next_b, other_ffn_a, other_ffn_b = loosely(
+        middle, two_a, two_b, next_a, next_b, other_ffn_a, other_ffn_b
+    )
+    ffn_all = [ffn_a, next_a, other_ffn_a, exchanged_part(next_a, 1 << CORE)]
+    ffn_all += [ffn_b, next_b, other_ffn_b, exchanged_part(next_b, 1 << CORE)]
     packed = ((HALF, FFN_A), BF16)
-    layer_out, keep_a, send_a, keep_b, send_b, mid_grad, ffn_gg = call(
+    whole = ((DEPTH, FFN_A), BF16)
+    gate_up = ((DEPTH, FF + FF // 4), BF16)
+    wide = ((BLK, FF), BF16)
+    layer_out, keep_a, send_a, keep_b, send_b, gate_g, up_g, ffn_out_gg = call(
         ffn_kernel,
-        [((BLK, D), BF16), packed, packed, packed, packed, ((BLK, D), F32), ((2, D), F32)],
-        [where, middle, cotangent, gain_d, perm_a, perm_b, two_a, two_b]
-        + [ffn_a, ffn_other_a, ffn_b, ffn_other_b],
+        [((BLK, D), BF16), packed, packed, packed, packed, wide, wide, ((1, D), F32)],
+        [where, middle, cotangent, gain_d, two_a, two_b] + ffn_all,
         [
+            whole,
+            whole,
             ((FF, D), BF16),
             ((FF, D), BF16),
             ((BLK, FF), F32),
             ((BLK, FF), F32),
-            ((BLK, FF), BF16),
-            ((BLK, FF), BF16),
-            ((BLK, FF), BF16),
-            (rows, F32),
-            (rows, F32),
+            wide,
+            ((2 * DEPTH, BLK), BF16),
+            ((2 * DEPTH, BLK), BF16),
         ],
         scalars=1,
-        flops=1e6,
-    )
-    ffn_a = reduce_step((keep_a, send_a), CORE)
-    ffn_b = reduce_step((keep_b, send_b), CORE)
-    mid_grad_then, ffn_a, ffn_b = together(mid_grad, ffn_a, ffn_b)
+        left=8,
+    )
+    mid_grad, ffn_in_gg = call(
+        ffn_back_kernel,
+        [((BLK, D), F32), ((1, D), F32)],
+        [middle, cotangent, gain_d, perm_a, perm_b, gate_g, up_g] + ffn_all,
+        [gate_up, gate_up],
+        left=8,
+    )
+    came_a, came_b = exchanged_part(send_a, 1 << CORE), exchanged_part(send_b, 1 << CORE)
+    mid_grad, came_a, came_b = together(mid_grad, came_a, came_b)
+    keep_a, send_a = halved(added(keep_a, came_a))
+    keep_b, send_b = halved(added(keep_b, came_b))
+    cut = FF + FF // 4
+    came_a = exchanged_part(send_a[:, :cut], 1 << ORDER_A[1])
+    came_b = exchanged_part(send_b[:, :cut], 1 << ORDER_B[1])
     sixteen = ((HALF, QW + QW // 4), BF16)
     (
         kv_earlier,
@@ -714,77 +821,70 @@
             ((1, D), F32),
             ((1, HD), F32),
         ],
-        [where, mid_grad_then, attn_proj, places, gain_d, gain_h, out_w, heads_out, query_low]
+        [where, mid_grad, attn_proj, places, gain_d, gain_h, out_w, heads_out, query_low]
         + [kv_all, log_total, query_raw, cos_rows, sin_rows, one_a, attn_a, other_a],
-        [((QW, D), BF16), ((SPAN, 2 * HD), F32), ((BLK, QW), BF16)],
+        [((QW, D), BF16), ((SPAN, 2 * HD), F32), ((BLK, QW), BF16), ((2 * DEPTH, BLK), BF16)],
         scalars=1,
-        flops=1e6,
-    )
-    ffn_a = reduce_step(ffn_a, ORDER_A[1])
-    ffn_b = reduce_step(ffn_b, ORDER_B[1])
-    kv_earlier, query_send, out_send, ffn_a, ffn_b = together(
-        kv_earlier, query_send, out_send, ffn_a, ffn_b
-    )
+        flops=7e9,
+    )
+    kv_earlier, query_send, out_send, came_a, came_b = together(
+        kv_earlier, query_send, out_send, came_a, came_b
+    )
+    came_a = [came_a, exchanged_part(send_a[:, cut:], 1 << ORDER_A[1])]
+    came_b = [came_b, exchanged_part(send_b[:, cut:], 1 << ORDER_B[1])]
     came = [
         passed_along(kv_earlier[(BACK - step) * BLK : (BACK - step + 1) * BLK], "seq", -step)
         for step in range(1, BACK + 1)
     ]
-    query_state = reduce_step((query_keep, query_send), CORE)
-    out_state = reduce_step((out_keep, out_send), CORE)
-    ffn_a = reduce_total(ffn_a, ORDER_A[0])
-    ffn_b = reduce_total(ffn_b, ORDER_B[0])
-    came, query_state, out_state, ffn_a, ffn_b = together(
-        came, query_state, out_state, ffn_a, ffn_b
-    )
-    input_grad, kv_keep, kv_send, attn_in_gg, key_gg = call(
+    keep_a, send_a = halved(added(keep_a, jnp.concatenate(came_a, axis=1)))
+    keep_b, send_b = halved(added(keep_b, jnp.concatenate(came_b, axis=1)))
+    came_a = exchanged_part(send_a, 1 << ORDER_A[0])
+    came_b = exchanged_part(send_b, 1 << ORDER_B[0])
+    came_query = exchanged_part(query_send, 1 << CORE)
+    came_out = exchanged_part(out_send, 1 << CORE)
+    came, came_a, came_b, came_query, came_out = loosely(
+        came, came_a, came_b, came_query, came_out
+    )
+    ffn_total = jnp.concatenate([added(keep_a, came_a), added(keep_b, came_b)], axis=1)
+    query_keep, query_send = halved(added(query_keep, came_query))
+    ffn_two = sent_z(ffn_total, 2)
+    came_query = exchanged_part(query_send, 1 << ORDER_A[1])
+    kv_width = 2 * HD + 2 * LANES
+    input_grad, kv_keep, kv_send = call(
         input_kernel,
-        [
-            ((BLK, D), F32),
-            ((HALF, 2 * HD + LANES), BF16),
-            ((HALF, 2 * HD + LANES), BF16),
-            ((1, D), F32),
-            ((1, HD), F32),
-        ],
-        [tokens, mid_grad, gain_d, gain_h, perm_a, perm_b, one_b, attn_b, other_b]
-        + [kv_own]
+        [((BLK, D), F32), ((HALF, kv_width), BF16), ((HALF, kv_width), BF16)],
+        [tokens, mid_grad, gain_d, gain_h, perm_a, perm_b, one_b, attn_b, other_b, kv_own]
         + came
-        + [key_raw, cos_rows, sin_rows, back_a],
-        flops=1e6,
-    )
-    query_state = reduce_step(query_state, ORDER_A[1])
-    out_state = reduce_step(out_state, ORDER_B[1])
-    ffn = [reduce_z(total, (1, 2)) for total in (ffn_a, ffn_b)]
-    kv_keep, kv_send, query_state, out_state, ffn = together(
-        kv_keep, kv_send, query_state, out_state, ffn
-    )
-    gains_grad = jnp.concatenate(
-        [attn_in_gg[0], attn_out_gg[0], ffn_gg[1], ffn_gg[0], query_gg[0], key_gg[0]]
-    )
-    gain_rows = lax.dot_general(
-        picked(SLOTS_B).astype(F32),
-        jnp.pad(gains_grad.reshape(PARTS, gain_each), ((0, 0), (0, LANES - gain_each))),
-        (((0,), (0,)), ((), ())),
-        precision=lax.Precision.HIGHEST,
-        preferred_element_type=F32,
-    ).astype(BF16)
-    kv_state = (
-        jnp.concatenate([kv_keep, gain_rows[:HALF]], axis=1),
-        jnp.concatenate([kv_send, gain_rows[HALF:]], axis=1),
-    )
-    kv_state = reduce_step(reduce_step(kv_state, CORE), ORDER_B[1])
-    query_total = reduce_total(query_state, ORDER_A[0])
-    out_total = reduce_total(out_state, ORDER_B[0])
-    ffn = [reduce_z(total, (3,), result) for total, result in zip((ffn_a, ffn_b), ffn)]
-    kv_state, query_total, out_total, ffn = together(kv_state, query_total, out_total, ffn)
-    kv_total = reduce_total(kv_state, ORDER_B[0])
-    query_sum = reduce_z(query_total, (1, 2, 3))
-    out_sum = reduce_z(out_total, (1, 2, 3))
-    kv_total, query_sum, out_sum = together(kv_total, query_sum, out_sum)
-    kv_sum = reduce_z(kv_total, (1, 2, 3))
+        + [key_raw, cos_rows, sin_rows, back_a, owners_b, fold]
+        + [attn_out_gg, ffn_out_gg, ffn_in_gg, query_gg],
+        [((2 * DEPTH, BLK), BF16)],
+        flops=5e9,
+    )
+    kv_send, ffn_two, came_query = loosely(kv_send, ffn_two, came_query)
+    came_kv = exchanged_part(kv_send, 1 << CORE)
+    ffn_one = sent_z(ffn_total, 1)
+    came_kv, ffn_one = loosely(came_kv, ffn_one)
+    rest_keep, rest_send = halved(
+        jnp.concatenate([added(out_keep, came_out), added(kv_keep, came_kv)], axis=1)
+    )
+    query_keep, query_send = halved(added(query_keep, came_query))
+    came_query = exchanged_part(query_send, 1 << ORDER_A[0])
+    came_rest = exchanged_part(rest_send, 1 << ORDER_B[1])
+    ffn_three = sent_z(ffn_total, 3)
+    came_query, came_rest, ffn_three = loosely(came_query, came_rest, ffn_three)
+    rest_keep, rest_send = halved(added(rest_keep, came_rest))
+    came_rest = exchanged_part(rest_send, 1 << ORDER_B[0])
+    (came_rest,) = loosely(came_rest)
+    attn_total = jnp.concatenate(
+        [added(query_keep, came_query), added(rest_keep, came_rest)], axis=1
+    )
+    attn_came = loosely(*(sent_z(attn_total, k) for k in range(1, 4)))
+    ffn_sum = ffn_total[:MAIN] + sum(c.astype(F32) for c in (ffn_one, ffn_two, ffn_three))
+    attn_sum = attn_total[:MAIN] + sum(c.astype(F32) for c in attn_came)
     flat = [((160, LANES), F32), ((40, LANES), F32), ((320, LANES), F32)]
-    grad_gate, grad_up, grad_down = call(unpack_ffn_kernel, [flat[2]] * 3, ffn)
+    grad_gate, grad_up, grad_down = call(unpack_ffn_kernel, [flat[2]] * 3, [ffn_sum])
     grad_query, grad_key, grad_value, grad_out = call(
-        unpack_attn_kernel, [flat[0], flat[1], flat[1], flat[0]], [query_sum, out_sum, kv_sum]
+        unpack_attn_kernel, [flat[0], flat[1], flat[1], flat[0]], [attn_sum]
     )
     return (
         layer_out,
@@ -799,7 +899,7 @@
                 grad_gate,
                 grad_up,
                 grad_down,
-                kv_sum[0, 2 * HD + LANES : 2 * HD + LANES + gain_each],
+                attn_sum[0, QW + QW // 4 + 2 * D + 2 * HD + LANES :][:gain_each],
             )
         ),
     )

time: 260 us -> 216 us (0.83)
  waiting for transfers between devices: 87.5 us -> 62.6 us
  starting transfers between devices: 70.5 us -> 49.9 us
  Pallas kernels: 65.2 us -> 72.6 us
  other arithmetic: 19.8 us -> 14 us
    ppermute x48 -> x41, waiting for transfers between devices: 80.5 us -> 53.6 us  [exchanged(): return lax.ppermute(value, AXES, [(i, i ^ mask) for i in range(count)])]
    ppermute x48 -> x41, starting transfers between devices: 57.3 us -> 41.5 us  [exchanged(): return lax.ppermute(value, AXES, [(i, i ^ mask) for i in range(count)])]
    pallas_call x8 -> x9, Pallas kernels: 65.2 us -> 72.6 us  [call(): pl.pallas_call(kernel, out_shape=shapes, in_specs=places, out_specs=[vmem...]
    ppermute x4, starting transfers between devices: 13.2 us -> 8.38 us  [passed_along(): lax.ppermute(value, axis, [(source, source + steps) for source in range(f...]
    concatenate x12 -> x6, other arithmetic: 3.49 us -> 0.33 us  [stacked(): return jnp.concatenate(pieces, axis=0)]
    add x13 -> x8, other arithmetic: 5.05 us -> 2.23 us  [the longest x1 0.94 us: local(): ffn_total[:MAIN]]
    unnamed x51 -> x52, local copies, waits for them, and re-layouts: 5.91 us -> 7.3 us
    another operation x15 -> x10, other arithmetic: 4.69 us -> 5.57 us
  transfers between devices with their start and end apart: 52 -> 45, of which waited for: 25 -> 17; matrix products, arithmetic and copies ran while one was open for 9% -> 7% of each run, Pallas kernels for 11% -> 22%
where the time goes in v1:
time: 216 us; the launch traced here: 215 us
  Pallas kernels  72.6 us (34%)
  waiting for transfers between devices  62.6 us (29%)
  starting transfers between devices  49.9 us (23%)
  local copies, waits for them, and re-layouts  14.8 us (7%)
  other arithmetic  14 us (6%)
    pallas_call x9, Pallas kernels, call(): pl.pallas_call(kernel, out_shape=shapes, in_specs=places, out_specs=[vmem...  72.6 us
    ppermute x41, waiting for transfers between devices, exchanged(): return lax.ppermute(value, AXES, [(i, i ^ mask) for i in range(count)])  53.6 us
    ppermute x41, starting transfers between devices, exchanged(): return lax.ppermute(value, AXES, [(i, i ^ mask) for i in range(count)])  41.5 us
    ppermute x4, waiting for transfers between devices, passed_along(): lax.ppermute(value, axis, [(source, source + steps) for source in range(f...  9.05 us
    ppermute x4, starting transfers between devices, passed_along(): lax.ppermute(value, axis, [(source, source + steps) for source in range(f...  8.38 us
    unnamed x52, local copies, waits for them, and re-layouts  7.3 us
    another operation x10, other arithmetic  5.57 us
  transfers between devices with their start and end apart: 45, of which 17 were waited for; matrix products, arithmetic and copies ran while one was open for 7% of the time, Pallas kernels for 22%

profile of v1, /device:TPU:0, one launch (start us, length us, event | category | flops | bytes accessed | tf_op | source)
XLA Modules:
  0.0 215.3 jit_solution(2418570561841563530)
XLA Ops:
  0.7 1.3 pad.4.gains
  1.9 1.9 shard_map.213
  3.9 3.0 %collective-permute-start = (bf16[16,3328]{1,0:T(8,128)(2,1)}, bf16[16,3328]{1,0:T(8,128)(2,1)S(1)}, u32[]{:S(2)}, u32[]{:S(2)}) collective-permute-start(bf16[16,3328]{1,0:T(8,128)(2,1)} %get-tuple-element.71), channel_id=1, source_target_pairs={{0,2},{1,3},{2,0},{3,1},{4,6},{5,7},{6,4},{7,5},{8,10},{9,11},{10,... | collective-permute-start | bytes 319496 | tf_op jit(solution)/shard_map/ppermute | solution.py:57
  6.9 2.6 %collective-permute-start.1 = (bf16[16,3328]{1,0:T(8,128)(2,1)}, bf16[16,3328]{1,0:T(8,128)(2,1)S(1)}, u32[]{:S(2)}, u32[]{:S(2)}) collective-permute-start(bf16[16,3328]{1,0:T(8,128)(2,1)} %get-tuple-element.71), channel_id=1, source_target_pairs={{0,4},{1,5},{2,6},{3,7},{4,0},{5,1},{6,2},{7,3},{8,12},{9,13},{10,... | collective-permute-start | bytes 319496 | tf_op jit(solution)/shard_map/ppermute | solution.py:57
  10.5 1.5 fusion.perm_a
  12.2 1.6 fusion.1.perm_b
  13.8 1.2 multiply_sine_fusion
  15.8 2.4 %collective-permute-done.1 = bf16[16,3328]{1,0:T(8,128)(2,1)S(1)} collective-permute-done((bf16[16,3328]{1,0:T(8,128)(2,1)}, bf16[16,3328]{1,0:T(8,128)(2,1)S(1)}, u32[]{:S(2)}, u32[]{:S(2)}) %collective-permute-start.1) | collective-permute-done | bytes 106528 | tf_op jit(solution)/shard_map/ppermute | solution.py:57
  18.3 1.6 collective-permute-start.3
  19.8 1.5 collective-permute-start.6
  21.4 1.8 collective-permute-start.11
  23.1 1.3 collective-permute-start.12
  24.5 1.4 collective-permute-start.13
  27.1 3.6 %collective-permute-done.11 = bf16[16,7680]{1,0:T(8,128)(2,1)S(1)} collective-permute-done((bf16[16,7680]{1,0:T(8,128)(2,1)S(1)}, bf16[16,7680]{1,0:T(8,128)(2,1)S(1)}, u32[]{:S(2)}, u32[]{:S(2)}) %collective-permute-start.11) | collective-permute-done | bytes 245792 | tf_op jit(solution)/shard_map/ppermute | solution.py:57
  30.7 12.2 %collective-permute-done.12 = bf16[16,7680]{1,0:T(8,128)(2,1)S(1)} collective-permute-done((bf16[16,7680]{1,0:T(8,128)(2,1)S(1)}, bf16[16,7680]{1,0:T(8,128)(2,1)S(1)}, u32[]{:S(2)}, u32[]{:S(2)}) %collective-permute-start.12) | collective-permute-done | bytes 245792 | tf_op jit(solution)/shard_map/ppermute | solution.py:57
  44.9 9.7 %collective-permute-done.14 = bf16[64,3840]{1,0:T(8,128)(2,1)S(1)} collective-permute-done((bf16[64,3840]{1,0:T(8,128)(2,1)S(1)}, bf16[64,3840]{1,0:T(8,128)(2,1)S(1)}, u32[]{:S(2)}, u32[]{:S(2)}) %collective-permute-start.14) | collective-permute-done | bytes 491552 | tf_op jit(solution)/shard_map/ppermute | solution.py:57
  55.1 2.2 %collective-permute-done.18 = bf16[64,3840]{1,0:T(8,128)(2,1)S(1)} collective-permute-done((bf16[64,3840]{1,0:T(8,128)(2,1)S(1)}, bf16[64,3840]{1,0:T(8,128)(2,1)S(1)}, u32[]{:S(2)}, u32[]{:S(2)}) %collective-permute-start.18) | collective-permute-done | bytes 491552 | tf_op jit(solution)/shard_map/ppermute | solution.py:57
  57.3 1.6 collective-permute-start.19
  58.9 0.9 copy-done.19
  60.1 6.9 %shard_map.214 = (bf16[256,1024]{1,0:T(8,128)(2,1)}, bf16[256,512]{1,0:T(8,128)(2,1)}, f32[256,1024]{1,0:T(8,128)}, f32[256,256]{1,0:T(8,128)}, bf16[256,1024]{1...) custom-call(bf16[256,640]{1,0:T(8,128)(2,1)} %tokens.5, s32[32,1]{1,0:T(8,128)} %copy.26.owners, ...), custom_call_target="tpu_custom_call" | custom-call | flops 8999999488 | tf_op jit(solution)/shard_map/pallas_call | solution.py:604
  67.1 3.6 %collective-permute-start.9 = (bf16[256,512]{1,0:T(8,128)(2,1)}, bf16[256,512]{1,0:T(8,128)(2,1)S(1)}, u32[]{:S(2)}, u32[]{:S(2)}) collective-permute-start(bf16[256,512]{1,0:T(8,128)(2,1)} %get-tuple-element.77), channel_id=1, source_target_pairs={{0,2},{1,3},{2,4},{3,5},{4,6},{5,7},{8,10},{9,11},{10,12},{11,13},... | collective-permute-start | bytes 786440 | tf_op jit(solution)/shard_map/ppermute | solution.py:67
  70.7 2.2 %collective-permute-start.10 = (bf16[256,512]{1,0:T(8,128)(2,1)}, bf16[256,512]{1,0:T(8,128)(2,1)S(1)}, u32[]{:S(2)}, u32[]{:S(2)}) collective-permute-start(bf16[256,512]{1,0:T(8,128)(2,1)} %get-tuple-element.77), channel_id=1, source_target_pairs={{0,1},{1,2},{2,3},{3,4},{4,5},{5,6},{6,7},{8,9},{9,10},{10,11},{11... | collective-permute-start | bytes 786440 | tf_op jit(solution)/shard_map/ppermute | solution.py:67
  72.9 0.8 copy.27.positions
  75.5 1.4 collective-permute-done.10
  76.9 1.0 constant_dynamic-update-slice_fusion.4.kv_all
  77.9 0.9 copy-done.16
  78.7 7.6 %shard_map.215 = (bf16[256,1024]{1,0:T(8,128)(2,1)}, f32[256,512]{1,0:T(8,128)}, f32[256,640]{1,0:T(8,128)}, f32[256,640]{1,0:T(8,128)}, bf16[256,1024]{1,0:T(8,...) custom-call(s32[2]{0:T(128)} %pad_add_fusion.2.where, bf16[256,640]{1,0:T(8,128)(2,1)} %tokens.5, ...), custom_call_target="tpu_custom_call" | custom-call | flops 8999999488 | tf_op jit(solution)/shard_map/pallas_call | solution.py:604
  86.4 0.9 copy-done.3
  88.4 20.9 %shard_map.216 = (bf16[256,640]{1,0:T(8,128)(2,1)}, bf16[256,3840]{1,0:T(8,128)(2,1)}, bf16[256,3840]{1,0:T(8,128)(2,1)}, bf16[256,3840]{1,0:T(8,128)(2,1)}, bf1...) custom-call(s32[2]{0:T(128)} %pad_add_fusion.2.where, ...), custom_call_target="tpu_custom_call" | custom-call | flops 1000000 | tf_op jit(solution)/shard_map/pallas_call | solution.py:604
  110.5 11.0 %shard_map.217 = (f32[256,640]{1,0:T(8,128)}, f32[1,640]{1,0:T(1,128)}) custom-call(f32[256,640]{1,0:T(8,128)} %get-tuple-element.78.middle, bf16[256,640]{1,0:T(8,128)(2,1)} %cotangent.3, f32[4,640]{1,0:T(4,128)} %get-tuple-element.75.gain_d, bf16[640,1024]{1,0:T(8,128)(2,1)} %fusion.perm_a, bf16[640,1024]{1,0:T(8,128)(2,1)} %fusion.1.perm_b, ...), custom_call_target="tpu_custom_call" | custom-call | flops 1000000 | tf_op jit(solution)/shard_map/pallas_call | solution.py:604
  121.5 2.0 add_convert_fusion.1
  123.6 1.5 copy-done.7
  125.7 0.8 collective-permute-start.24
  126.5 3.0 %collective-permute-start.25 = (bf16[128,2560]{1,0:T(8,128)(2,1)S(1)}, bf16[128,2560]{1,0:T(8,128)(2,1)S(1)}, u32[]{:S(2)}, u32[]{:S(2)}) collective-permute-start(bf16[128,2560]{1,0:T(8,128)(2,1)S(1)} %slice.171), channel_id=1, source_target_pairs={{0,1},{1,0},{2,3},{3,2},{4,5},{5,4},{6,7},{7,6},{8,9},{9,8},{10,11... | collective-permute-start | bytes 1966088 | tf_op jit(solution)/shard_map/ppermute | solution.py:57
  129.5 1.3 collective-permute-start.38
  130.8 12.6 %shard_map.218 = (bf16[512,512]{1,0:T(8,128)(2,1)}, f32[256,512]{1,0:T(8,128)}, bf16[256,1280]{1,0:T(8,128)(2,1)}, bf16[256,1280]{1,0:T(8,128)(2,1)}, bf16[256,1...) custom-call(s32[2]{0:T(128)} %pad_add_fusion.2.where, ...), custom_call_target="tpu_custom_call" | custom-call | flops 7000000000 | tf_op jit(solution)/shard_map/pallas_call | solution.py:604
  143.4 1.7 collective-permute-done.25
  145.1 1.1 fusion.10
  146.1 1.3 collective-permute-start.26
  147.4 1.3 collective-permute-start.27
  148.8 0.8 collective-permute-done.38
  149.6 1.2 add_convert_fusion.3
  150.8 1.3 collective-permute-done.40
  152.2 1.8 collective-permute-start.39
  154.0 1.2 add_convert_fusion.2
  155.2 2.5 %collective-permute-done.26.came_one = bf16[256,512]{1,0:T(8,128)(2,1)S(1)} collective-permute-done((bf16[256,512]{1,0:T(8,128)(2,1)S(1)}, bf16[256,512]{1,0:T(8,128)(2,1)S(1)}, u32[]{:S(2)}, u32[]{:S(2)}) %collective-permute-start.26) | collective-permute-done | bytes 262176 | tf_op jit(solution)/shard_map/ppermute | solution.py:67
  157.7 1.3 collective-permute-start.41
  159.0 5.2 %collective-permute-done.27.came_two = bf16[256,512]{1,0:T(8,128)(2,1)S(1)} collective-permute-done((bf16[256,512]{1,0:T(8,128)(2,1)S(1)}, bf16[256,512]{1,0:T(8,128)(2,1)S(1)}, u32[]{:S(2)}, u32[]{:S(2)}) %collective-permute-start.27) | collective-permute-done | bytes 262176 | tf_op jit(solution)/shard_map/ppermute | solution.py:67
  164.9 8.2 %shard_map.219 = (f32[256,640]{1,0:T(8,128)}, bf16[256,768]{1,0:T(8,128)(2,1)}, bf16[256,768]{1,0:T(8,128)(2,1)}) custom-call(bf16[256,640]{1,0:T(8,128)(2,1)} %tokens.5, f32[256,640]{1,0:T(8,128)} %get-tuple-element.88.mid_grad, f32[4,640]{1,0:T(4,128)} %get-tuple-element.75.gain_d, f32[2,256]{1,0:T(2,128)} %get-tuple-element.89.gain_h, ...), custom_call_target="tpu_custom_call" | custom-call | flops 5000000000 | tf_op jit(solution)/shard_map/pallas_call | solution.py:604
  173.5 0.9 copy-done.12
  174.6 1.1 collective-permute-start.29
  176.4 5.3 %collective-permute-start.44 = (bf16[16,7680]{1,0:T(8,128)(2,1)S(1)}, bf16[16,7680]{1,0:T(8,128)(2,1)S(1)}, u32[]{:S(2)}, u32[]{:S(2)}) collective-permute-start(bf16[16,7680]{1,0:T(8,128)(2,1)S(1)} %get-tuple-element.129), channel_id=1, source_target_pairs={{0,6},{1,7},{2,4},{3,5},{4,2},{5,3},{6,0},{7,1},{8,14},{9,15},{10,... | collective-permute-start | bytes 737288 | tf_op jit(solution)/shard_map/ppermute | solution.py:57
  182.3 2.5 %collective-permute-done.29 = bf16[128,1280]{1,0:T(8,128)(2,1)S(1)} collective-permute-done((bf16[128,1280]{1,0:T(8,128)(2,1)S(1)}, bf16[128,1280]{1,0:T(8,128)(2,1)S(1)}, u32[]{:S(2)}, u32[]{:S(2)}) %collective-permute-start.29) | collective-permute-done | bytes 327712 | tf_op jit(solution)/shard_map/ppermute | solution.py:57
  185.0 6.1 %collective-permute-done.33 = bf16[128,2048]{1,0:T(8,128)(2,1)S(1)} collective-permute-done((bf16[128,2048]{1,0:T(8,128)(2,1)S(1)}, bf16[128,2048]{1,0:T(8,128)(2,1)S(1)}, u32[]{:S(2)}, u32[]{:S(2)}) %collective-permute-start.33) | collective-permute-done | bytes 524320 | tf_op jit(solution)/shard_map/ppermute | solution.py:57
  191.2 1.0 collective-permute-start.34
  192.3 1.6 collective-permute-done.30
  193.9 4.3 %collective-permute-done.34 = bf16[64,2048]{1,0:T(8,128)(2,1)S(1)} collective-permute-done((bf16[64,2048]{1,0:T(8,128)(2,1)S(1)}, bf16[64,2048]{1,0:T(8,128)(2,1)S(1)}, u32[]{:S(2)}, u32[]{:S(2)}) %collective-permute-start.34) | collective-permute-done | bytes 262176 | tf_op jit(solution)/shard_map/ppermute | solution.py:57
  198.3 4.3 %collective-permute-start.37 = (bf16[16,3328]{1,0:T(8,128)(2,1)S(1)}, bf16[16,3328]{1,0:T(8,128)(2,1)S(1)}, u32[]{:S(2)}, u32[]{:S(2)}) collective-permute-start(bf16[16,3328]{1,0:T(8,128)(2,1)S(1)} %get-tuple-element.136), channel_id=1, source_target_pairs={{0,6},{1,7},{2,4},{3,5},{4,2},{5,3},{6,0},{7,1},{8,14},{9,15},{10,... | collective-permute-start | bytes 319496 | tf_op jit(solution)/shard_map/ppermute | solution.py:57
  203.8 0.9 fusion.5.part
  204.7 1.9 shard_map.221
  206.6 5.1 %collective-permute-done.36 = bf16[16,3328]{1,0:T(8,128)(2,1)S(1)} collective-permute-done((bf16[16,3328]{1,0:T(8,128)(2,1)S(1)}, bf16[16,3328]{1,0:T(8,128)(2,1)S(1)}, u32[]{:S(2)}, u32[]{:S(2)}) %collective-permute-start.36) | collective-permute-done | bytes 106528 | tf_op jit(solution)/shard_map/ppermute | solution.py:57
  211.7 0.8 fusion.7.part
  212.5 1.6 shard_map.220
  214.1 1.2 slice_bitcast_fusion
  (152 shorter events, 15.1 us)
Async XLA Ops:
  0.6 13.2 %copy-start.17 = (s32[256]{0:T(256)S(1)}, s32[256]{0:T(256)}, u32[]{:S(2)}) copy-start(s32[256]{0:T(256)} %param.15) | copy-start | bytes 3076
  3.9 14.3 %copy-start.15 = (bf16[16,3328]{1,0:T(8,128)(2,1)S(1)}, bf16[16,3328]{1,0:T(8,128)(2,1)}, u32[]{:S(2)}) copy-start(bf16[16,3328]{1,0:T(8,128)(2,1)} %get-tuple-element.71) | copy-start | bytes 319492
  3.9 11.9 %collective-permute-start = (bf16[16,3328]{1,0:T(8,128)(2,1)}, bf16[16,3328]{1,0:T(8,128)(2,1)S(1)}, u32[]{:S(2)}, u32[]{:S(2)}) collective-permute-start(bf16[16,3328]{1,0:T(8,128)(2,1)} %get-tuple-element.71), channel_id=1, source_target_pairs={{0,2},{1,3},{2,0},{3,1},{4,6},{5,7},{6,4},{7,5},{8,10},{9,11},{10,... | collective-permute-start | bytes 319496 | tf_op jit(solution)/shard_map/ppermute | solution.py:57
  6.9 11.3 %collective-permute-start.1 = (bf16[16,3328]{1,0:T(8,128)(2,1)}, bf16[16,3328]{1,0:T(8,128)(2,1)S(1)}, u32[]{:S(2)}, u32[]{:S(2)}) collective-permute-start(bf16[16,3328]{1,0:T(8,128)(2,1)} %get-tuple-element.71), channel_id=1, source_target_pairs={{0,4},{1,5},{2,6},{3,7},{4,0},{5,1},{6,2},{7,3},{8,12},{9,13},{10,... | collective-permute-start | bytes 319496 | tf_op jit(solution)/shard_map/ppermute | solution.py:57
  9.5 8.7 %collective-permute-start.2 = (bf16[16,3328]{1,0:T(8,128)(2,1)}, bf16[16,3328]{1,0:T(8,128)(2,1)S(1)}, u32[]{:S(2)}, u32[]{:S(2)}) collective-permute-start(bf16[16,3328]{1,0:T(8,128)(2,1)} %get-tuple-element.71), channel_id=1, source_target_pairs={{0,6},{1,7},{2,4},{3,5},{4,2},{5,3},{6,0},{7,1},{8,14},{9,15},{10,... | collective-permute-start | bytes 319496 | tf_op jit(solution)/shard_map/ppermute | solution.py:57
  12.0 9.4 %copy-start.14 = (bf16[16,7680]{1,0:T(8,128)(2,1)S(1)}, bf16[16,7680]{1,0:T(8,128)(2,1)}, u32[]{:S(2)}) copy-start(bf16[16,7680]{1,0:T(8,128)(2,1)} %get-tuple-element.81) | copy-start | bytes 737284
  18.3 7.6 %collective-permute-start.3 = (bf16[64,1408]{1,0:T(8,128)(2,1)S(1)}, bf16[64,1408]{1,0:T(8,128)(2,1)S(1)}, u32[]{:S(2)}, u32[]{:S(2)}) collective-permute-start(bf16[64,1408]{1,0:T(8,128)(2,1)S(1)} %slice.166), channel_id=1, source_target_pairs={{0,1},{1,0},{2,3},{3,2},{4,5},{5,4},{6,7},{7,6},{8,9},{9,8},{10,11... | collective-permute-start | bytes 540680 | tf_op jit(solution)/shard_map/ppermute | solution.py:57
  19.8 6.6 %collective-permute-start.6 = (bf16[64,1920]{1,0:T(8,128)(2,1)S(1)}, bf16[64,1920]{1,0:T(8,128)(2,1)S(1)}, u32[]{:S(2)}, u32[]{:S(2)}) collective-permute-start(bf16[64,1920]{1,0:T(8,128)(2,1)S(1)} %slice.167), channel_id=1, source_target_pairs={{0,16},{1,17},{2,18},{3,19},{4,20},{5,21},{6,22},{7,23},{8,24},{9,... | collective-permute-start | bytes 737288 | tf_op jit(solution)/shard_map/ppermute | solution.py:57
  21.4 9.3 %collective-permute-start.11 = (bf16[16,7680]{1,0:T(8,128)(2,1)S(1)}, bf16[16,7680]{1,0:T(8,128)(2,1)S(1)}, u32[]{:S(2)}, u32[]{:S(2)}) collective-permute-start(bf16[16,7680]{1,0:T(8,128)(2,1)S(1)} %copy-done.14), channel_id=1, source_target_pairs={{0,2},{1,3},{2,0},{3,1},{4,6},{5,7},{6,4},{7,5},{8,10},{9,11},{10,... | collective-permute-start | bytes 737288 | tf_op jit(solution)/shard_map/ppermute | solution.py:57
  23.1 19.7 %collective-permute-start.12 = (bf16[16,7680]{1,0:T(8,128)(2,1)S(1)}, bf16[16,7680]{1,0:T(8,128)(2,1)S(1)}, u32[]{:S(2)}, u32[]{:S(2)}) collective-permute-start(bf16[16,7680]{1,0:T(8,128)(2,1)S(1)} %copy-done.14), channel_id=1, source_target_pairs={{0,4},{1,5},{2,6},{3,7},{4,0},{5,1},{6,2},{7,3},{8,12},{9,13},{10,... | collective-permute-start | bytes 737288 | tf_op jit(solution)/shard_map/ppermute | solution.py:57
  24.5 18.4 %collective-permute-start.13 = (bf16[16,7680]{1,0:T(8,128)(2,1)S(1)}, bf16[16,7680]{1,0:T(8,128)(2,1)S(1)}, u32[]{:S(2)}, u32[]{:S(2)}) collective-permute-start(bf16[16,7680]{1,0:T(8,128)(2,1)S(1)} %copy-done.14), channel_id=1, source_target_pairs={{0,6},{1,7},{2,4},{3,5},{4,2},{5,3},{6,0},{7,1},{8,14},{9,15},{10,... | collective-permute-start | bytes 737288 | tf_op jit(solution)/shard_map/ppermute | solution.py:57
  25.9 18.4 %collective-permute-start.4 = (bf16[128,1408]{1,0:T(8,128)(2,1)S(1)}, bf16[128,1408]{1,0:T(8,128)(2,1)S(1)}, u32[]{:S(2)}, u32[]{:S(2)}) collective-permute-start(bf16[128,1408]{1,0:T(8,128)(2,1)S(1)} %pad_maximum_fusion.7), channel_id=1, source_target_pairs={{0,16},{1,17},{2,18},{3,19},{4,20},{5,21},{6,22},{7,23},{8,24},{9,... | collective-permute-start | bytes 1081352 | tf_op jit(solution)/shard_map/ppermute | solution.py:57
  26.5 17.6 %collective-permute-start.7 = (bf16[128,1920]{1,0:T(8,128)(2,1)S(1)}, bf16[128,1920]{1,0:T(8,128)(2,1)S(1)}, u32[]{:S(2)}, u32[]{:S(2)}) collective-permute-start(bf16[128,1920]{1,0:T(8,128)(2,1)S(1)} %pad_maximum_fusion.6), channel_id=1, source_target_pairs={{0,1},{1,0},{2,3},{3,2},{4,5},{5,4},{6,7},{7,6},{8,9},{9,8},{10,11... | collective-permute-start | bytes 1474568 | tf_op jit(solution)/shard_map/ppermute | solution.py:57
  43.0 11.6 %collective-permute-start.14 = (bf16[64,3840]{1,0:T(8,128)(2,1)S(1)}, bf16[64,3840]{1,0:T(8,128)(2,1)S(1)}, u32[]{:S(2)}, u32[]{:S(2)}) collective-permute-start(bf16[64,3840]{1,0:T(8,128)(2,1)S(1)} %get-tuple-element.132), channel_id=1, source_target_pairs={{0,1},{1,0},{2,3},{3,2},{4,5},{5,4},{6,7},{7,6},{8,9},{9,8},{10,11... | collective-permute-start | bytes 1474568 | tf_op jit(solution)/shard_map/ppermute | solution.py:57
  43.6 13.6 %collective-permute-start.18 = (bf16[64,3840]{1,0:T(8,128)(2,1)S(1)}, bf16[64,3840]{1,0:T(8,128)(2,1)S(1)}, u32[]{:S(2)}, u32[]{:S(2)}) collective-permute-start(bf16[64,3840]{1,0:T(8,128)(2,1)S(1)} %get-tuple-element.131), channel_id=1, source_target_pairs={{0,16},{1,17},{2,18},{3,19},{4,20},{5,21},{6,22},{7,23},{8,24},{9,... | collective-permute-start | bytes 1474568 | tf_op jit(solution)/shard_map/ppermute | solution.py:57
  44.2 13.1 %copy-start.9 = (bf16[256,1920]{1,0:T(8,128)(2,1)}, bf16[256,1920]{1,0:T(8,128)(2,1)S(1)}, u32[]{:S(2)}) copy-start(bf16[256,1920]{1,0:T(8,128)(2,1)S(1)} %pad_maximum_fusion.2.mine_b) | copy-start | bytes 2949124
  44.2 14.7 %collective-permute-start.8 = (bf16[256,1920]{1,0:T(8,128)(2,1)S(1)}, bf16[256,1920]{1,0:T(8,128)(2,1)S(1)}, u32[]{:S(2)}, u32[]{:S(2)}) collective-permute-start(bf16[256,1920]{1,0:T(8,128)(2,1)S(1)} %pad_maximum_fusion.2.mine_b), channel_id=1, source_target_pairs={{0,8},{1,9},{2,10},{3,11},{4,12},{5,13},{6,14},{7,15},{8,0},{9,1},... | collective-permute-start | bytes 2949128 | tf_op jit(solution)/shard_map/ppermute | solution.py:57
  44.3 13.0 %copy-start.10 = (bf16[256,1408]{1,0:T(8,128)(2,1)}, bf16[256,1408]{1,0:T(8,128)(2,1)S(1)}, u32[]{:S(2)}) copy-start(bf16[256,1408]{1,0:T(8,128)(2,1)S(1)} %pad_maximum_fusion.5.mine_a) | copy-start | bytes 2162692
  44.4 14.5 %collective-permute-start.5 = (bf16[256,1408]{1,0:T(8,128)(2,1)S(1)}, bf16[256,1408]{1,0:T(8,128)(2,1)S(1)}, u32[]{:S(2)}, u32[]{:S(2)}) collective-permute-start(bf16[256,1408]{1,0:T(8,128)(2,1)S(1)} %pad_maximum_fusion.5.mine_a), channel_id=1, source_target_pairs={{0,8},{1,9},{2,10},{3,11},{4,12},{5,13},{6,14},{7,15},{8,0},{9,1},... | collective-permute-start | bytes 2162696 | tf_op jit(solution)/shard_map/ppermute | solution.py:57
  54.7 19.7 %copy-start = (bf16[128,3840]{1,0:T(8,128)(2,1)}, bf16[128,3840]{1,0:T(8,128)(2,1)S(1)}, u32[]{:S(2)}) copy-start(bf16[128,3840]{1,0:T(8,128)(2,1)S(1)} %pad_maximum_fusion.3.a_0) | copy-start | bytes 2949124
  54.7 19.6 %collective-permute-start.15 = (bf16[128,3840]{1,0:T(8,128)(2,1)S(1)}, bf16[128,3840]{1,0:T(8,128)(2,1)S(1)}, u32[]{:S(2)}, u32[]{:S(2)}) collective-permute-start(bf16[128,3840]{1,0:T(8,128)(2,1)S(1)} %pad_maximum_fusion.3.a_0), channel_id=1, source_target_pairs={{0,16},{1,17},{2,18},{3,19},{4,20},{5,21},{6,22},{7,23},{8,24},{9,... | collective-permute-start | bytes 2949128 | tf_op jit(solution)/shard_map/ppermute | solution.py:57
  57.3 17.0 %copy-start.1 = (bf16[128,3840]{1,0:T(8,128)(2,1)}, bf16[128,3840]{1,0:T(8,128)(2,1)S(1)}, u32[]{:S(2)}) copy-start(bf16[128,3840]{1,0:T(8,128)(2,1)S(1)} %pad_maximum_fusion.4.b_0) | copy-start | bytes 2949124
  57.3 17.6 %collective-permute-start.19 = (bf16[128,3840]{1,0:T(8,128)(2,1)S(1)}, bf16[128,3840]{1,0:T(8,128)(2,1)}, u32[]{:S(2)}, u32[]{:S(2)}) collective-permute-start(bf16[128,3840]{1,0:T(8,128)(2,1)S(1)} %pad_maximum_fusion.4.b_0), channel_id=1, source_target_pairs={{0,1},{1,0},{2,3},{3,2},{4,5},{5,4},{6,7},{7,6},{8,9},{9,8},{10,11... | collective-permute-start | bytes 2949128 | tf_op jit(solution)/shard_map/ppermute | solution.py:57
  58.9 1.2 copy-start.18
  67.1 8.0 %collective-permute-start.9 = (bf16[256,512]{1,0:T(8,128)(2,1)}, bf16[256,512]{1,0:T(8,128)(2,1)S(1)}, u32[]{:S(2)}, u32[]{:S(2)}) collective-permute-start(bf16[256,512]{1,0:T(8,128)(2,1)} %get-tuple-element.77), channel_id=1, source_target_pairs={{0,2},{1,3},{2,4},{3,5},{4,6},{5,7},{8,10},{9,11},{10,12},{11,13},... | collective-permute-start | bytes 786440 | tf_op jit(solution)/shard_map/ppermute | solution.py:67
  70.7 6.2 %collective-permute-start.10 = (bf16[256,512]{1,0:T(8,128)(2,1)}, bf16[256,512]{1,0:T(8,128)(2,1)S(1)}, u32[]{:S(2)}, u32[]{:S(2)}) collective-permute-start(bf16[256,512]{1,0:T(8,128)(2,1)} %get-tuple-element.77), channel_id=1, source_target_pairs={{0,1},{1,2},{2,3},{3,4},{4,5},{5,6},{6,7},{8,9},{9,10},{10,11},{11... | collective-permute-start | bytes 786440 | tf_op jit(solution)/shard_map/ppermute | solution.py:67
  74.4 12.0 %collective-permute-start.16 = (bf16[128,3840]{1,0:T(8,128)(2,1)S(1)}, bf16[128,3840]{1,0:T(8,128)(2,1)S(1)}, u32[]{:S(2)}, u32[]{:S(2)}) collective-permute-start(bf16[128,3840]{1,0:T(8,128)(2,1)S(1)} %pad_maximum_fusion.3.a_0), channel_id=1, source_target_pairs={{0,8},{1,9},{2,10},{3,11},{4,12},{5,13},{6,14},{7,15},{8,0},{9,1},... | collective-permute-start | bytes 2949128 | tf_op jit(solution)/shard_map/ppermute | solution.py:57
  74.4 12.0 %copy-start.2 = (bf16[128,3840]{1,0:T(8,128)(2,1)}, bf16[128,3840]{1,0:T(8,128)(2,1)S(1)}, u32[]{:S(2)}) copy-start(bf16[128,3840]{1,0:T(8,128)(2,1)S(1)} %collective-permute-done.15.a_1) | copy-start | bytes 2949124
  74.4 12.0 %collective-permute-start.20 = (bf16[128,3840]{1,0:T(8,128)(2,1)S(1)}, bf16[128,3840]{1,0:T(8,128)(2,1)S(1)}, u32[]{:S(2)}, u32[]{:S(2)}) collective-permute-start(bf16[128,3840]{1,0:T(8,128)(2,1)S(1)} %pad_maximum_fusion.4.b_0), channel_id=1, source_target_pairs={{0,8},{1,9},{2,10},{3,11},{4,12},{5,13},{6,14},{7,15},{8,0},{9,1},... | collective-permute-start | bytes 2949128 | tf_op jit(solution)/shard_map/ppermute | solution.py:57
  74.9 11.4 %collective-permute-start.17 = (bf16[128,3840]{1,0:T(8,128)(2,1)S(1)}, bf16[128,3840]{1,0:T(8,128)(2,1)S(1)}, u32[]{:S(2)}, u32[]{:S(2)}) collective-permute-start(bf16[128,3840]{1,0:T(8,128)(2,1)S(1)} %collective-permute-done.15.a_1), channel_id=1, source_target_pairs={{0,8},{1,9},{2,10},{3,11},{4,12},{5,13},{6,14},{7,15},{8,0},{9,1},... | collective-permute-start | bytes 2949128 | tf_op jit(solution)/shard_map/ppermute | solution.py:57
  75.0 11.4 %collective-permute-start.21 = (bf16[128,3840]{1,0:T(8,128)(2,1)}, bf16[128,3840]{1,0:T(8,128)(2,1)S(1)}, u32[]{:S(2)}, u32[]{:S(2)}) collective-permute-start(bf16[128,3840]{1,0:T(8,128)(2,1)} %collective-permute-done.19.b_1), channel_id=1, source_target_pairs={{0,8},{1,9},{2,10},{3,11},{4,12},{5,13},{6,14},{7,15},{8,0},{9,1},... | collective-permute-start | bytes 2949128 | tf_op jit(solution)/shard_map/ppermute | solution.py:57
  86.3 1.0 copy-start.3
  86.4 1.2 copy-start.4
  86.4 1.6 copy-start.5
  86.4 1.9 copy-start.6
  109.2 12.3 %collective-permute-start.22 = (bf16[256,3840]{1,0:T(8,128)(2,1)}, bf16[256,3840]{1,0:T(8,128)(2,1)}, u32[]{:S(2)}, u32[]{:S(2)}) collective-permute-start(bf16[256,3840]{1,0:T(8,128)(2,1)} %get-tuple-element.86), channel_id=1, source_target_pairs={{0,8},{1,9},{2,10},{3,11},{4,12},{5,13},{6,14},{7,15},{8,0},{9,1},... | collective-permute-start | bytes 5898248 | tf_op jit(solution)/shard_map/ppermute | solution.py:57
  109.3 12.2 %collective-permute-start.23 = (bf16[256,3840]{1,0:T(8,128)(2,1)}, bf16[256,3840]{1,0:T(8,128)(2,1)S(1)}, u32[]{:S(2)}, u32[]{:S(2)}) collective-permute-start(bf16[256,3840]{1,0:T(8,128)(2,1)} %get-tuple-element.87), channel_id=1, source_target_pairs={{0,8},{1,9},{2,10},{3,11},{4,12},{5,13},{6,14},{7,15},{8,0},{9,1},... | collective-permute-start | bytes 5898248 | tf_op jit(solution)/shard_map/ppermute | solution.py:57
  110.5 11.0 %copy-start.8 = (bf16[256,3840]{1,0:T(8,128)(2,1)S(1)}, bf16[256,3840]{1,0:T(8,128)(2,1)}, u32[]{:S(2)}) copy-start(bf16[256,3840]{1,0:T(8,128)(2,1)} %get-tuple-element.101) | copy-start | bytes 5898244
  123.5 1.5 copy-start.7
  125.7 17.7 %collective-permute-start.24 = (bf16[128,2560]{1,0:T(8,128)(2,1)S(1)}, bf16[128,2560]{1,0:T(8,128)(2,1)S(1)}, u32[]{:S(2)}, u32[]{:S(2)}) collective-permute-start(bf16[128,2560]{1,0:T(8,128)(2,1)S(1)} %slice.170), channel_id=1, source_target_pairs={{0,16},{1,17},{2,18},{3,19},{4,20},{5,21},{6,22},{7,23},{8,24},{9,... | collective-permute-start | bytes 1966088 | tf_op jit(solution)/shard_map/ppermute | solution.py:57
  126.5 18.6 %collective-permute-start.25 = (bf16[128,2560]{1,0:T(8,128)(2,1)S(1)}, bf16[128,2560]{1,0:T(8,128)(2,1)S(1)}, u32[]{:S(2)}, u32[]{:S(2)}) collective-permute-start(bf16[128,2560]{1,0:T(8,128)(2,1)S(1)} %slice.171), channel_id=1, source_target_pairs={{0,1},{1,0},{2,3},{3,2},{4,5},{5,4},{6,7},{7,6},{8,9},{9,8},{10,11... | collective-permute-start | bytes 1966088 | tf_op jit(solution)/shard_map/ppermute | solution.py:57
  129.5 20.1 %collective-permute-start.38 = (bf16[128,1280]{1,0:T(8,128)(2,1)S(1)}, bf16[128,1280]{1,0:T(8,128)(2,1)}, u32[]{:S(2)}, u32[]{:S(2)}) collective-permute-start(bf16[128,1280]{1,0:T(8,128)(2,1)S(1)} %slice.186), channel_id=1, source_target_pairs={{0,16},{1,17},{2,18},{3,19},{4,20},{5,21},{6,22},{7,23},{8,24},{9,... | collective-permute-start | bytes 983048 | tf_op jit(solution)/shard_map/ppermute | solution.py:57
  130.8 21.4 %collective-permute-start.40 = (bf16[128,1280]{1,0:T(8,128)(2,1)S(1)}, bf16[128,1280]{1,0:T(8,128)(2,1)}, u32[]{:S(2)}, u32[]{:S(2)}) collective-permute-start(bf16[128,1280]{1,0:T(8,128)(2,1)S(1)} %slice.190), channel_id=1, source_target_pairs={{0,1},{1,0},{2,3},{3,2},{4,5},{5,4},{6,7},{7,6},{8,9},{9,8},{10,11... | collective-permute-start | bytes 983048 | tf_op jit(solution)/shard_map/ppermute | solution.py:57
  146.1 11.6 %collective-permute-start.26 = (bf16[256,512]{1,0:T(8,128)(2,1)S(1)}, bf16[256,512]{1,0:T(8,128)(2,1)S(1)}, u32[]{:S(2)}, u32[]{:S(2)}) collective-permute-start(bf16[256,512]{1,0:T(8,128)(2,1)S(1)} %get-tuple-element.134), channel_id=1, source_target_pairs={{1,0},{2,1},{3,2},{4,3},{5,4},{6,5},{7,6},{9,8},{10,9},{11,10},{12... | collective-permute-start | bytes 786440 | tf_op jit(solution)/shard_map/ppermute | solution.py:67
  147.4 16.8 %collective-permute-start.27 = (bf16[256,512]{1,0:T(8,128)(2,1)S(1)}, bf16[256,512]{1,0:T(8,128)(2,1)S(1)}, u32[]{:S(2)}, u32[]{:S(2)}) collective-permute-start(bf16[256,512]{1,0:T(8,128)(2,1)S(1)} %get-tuple-element.133), channel_id=1, source_target_pairs={{2,0},{3,1},{4,2},{5,3},{6,4},{7,5},{10,8},{11,9},{12,10},{13,11},... | collective-permute-start | bytes 786440 | tf_op jit(solution)/shard_map/ppermute | solution.py:67
  148.7 27.1 %collective-permute-start.31 = (bf16[256,1280]{1,0:T(8,128)(2,1)}, bf16[256,1280]{1,0:T(8,128)(2,1)S(1)}, u32[]{:S(2)}, u32[]{:S(2)}) collective-permute-start(bf16[256,1280]{1,0:T(8,128)(2,1)} %get-tuple-element.116), channel_id=1, source_target_pairs={{0,8},{1,9},{2,10},{3,11},{4,12},{5,13},{6,14},{7,15},{8,0},{9,1},... | collective-permute-start | bytes 1966088 | tf_op jit(solution)/shard_map/ppermute | solution.py:57
  149.6 23.9 %collective-permute-start.28 = (bf16[256,1280]{1,0:T(8,128)(2,1)}, bf16[256,1280]{1,0:T(8,128)(2,1)S(1)}, u32[]{:S(2)}, u32[]{:S(2)}) collective-permute-start(bf16[256,1280]{1,0:T(8,128)(2,1)} %get-tuple-element.114), channel_id=1, source_target_pairs={{0,8},{1,9},{2,10},{3,11},{4,12},{5,13},{6,14},{7,15},{8,0},{9,1},... | collective-permute-start | bytes 1966088 | tf_op jit(solution)/shard_map/ppermute | solution.py:57
  152.2 20.9 %collective-permute-start.39 = (bf16[64,3840]{1,0:T(8,128)(2,1)S(1)}, bf16[64,3840]{1,0:T(8,128)(2,1)S(1)}, u32[]{:S(2)}, u32[]{:S(2)}) collective-permute-start(bf16[64,3840]{1,0:T(8,128)(2,1)S(1)} %slice.188), channel_id=1, source_target_pairs={{0,1},{1,0},{2,3},{3,2},{4,5},{5,4},{6,7},{7,6},{8,9},{9,8},{10,11... | collective-permute-start | bytes 1474568 | tf_op jit(solution)/shard_map/ppermute | solution.py:57
  157.7 7.2 %copy-start.20 = (bf16[256,512]{1,0:T(8,128)(2,1)}, bf16[256,512]{1,0:T(8,128)(2,1)S(1)}, u32[]{:S(2)}) copy-start(bf16[256,512]{1,0:T(8,128)(2,1)S(1)} %collective-permute-done.26.came_one) | copy-start | bytes 786436
  157.7 15.5 %collective-permute-start.41 = (bf16[64,3840]{1,0:T(8,128)(2,1)S(1)}, bf16[64,3840]{1,0:T(8,128)(2,1)S(1)}, u32[]{:S(2)}, u32[]{:S(2)}) collective-permute-start(bf16[64,3840]{1,0:T(8,128)(2,1)S(1)} %slice.192), channel_id=1, source_target_pairs={{0,16},{1,17},{2,18},{3,19},{4,20},{5,21},{6,22},{7,23},{8,24},{9,... | collective-permute-start | bytes 1474568 | tf_op jit(solution)/shard_map/ppermute | solution.py:57
  173.1 2.8 %collective-permute-start.32 = (bf16[256,768]{1,0:T(8,128)(2,1)}, bf16[256,768]{1,0:T(8,128)(2,1)S(1)}, u32[]{:S(2)}, u32[]{:S(2)}) collective-permute-start(bf16[256,768]{1,0:T(8,128)(2,1)} %get-tuple-element.118), channel_id=1, source_target_pairs={{0,8},{1,9},{2,10},{3,11},{4,12},{5,13},{6,14},{7,15},{8,0},{9,1},... | collective-permute-start | bytes 1179656 | tf_op jit(solution)/shard_map/ppermute | solution.py:57
  173.4 1.1 copy-start.12
  173.5 2.3 %copy-start.11 = (bf16[256,1280]{1,0:T(8,128)(2,1)S(1)}, bf16[256,1280]{1,0:T(8,128)(2,1)}, u32[]{:S(2)}) copy-start(bf16[256,1280]{1,0:T(8,128)(2,1)} %get-tuple-element.115) | copy-start | bytes 1966084
  174.4 1.5 copy-start.13
  174.6 10.2 %collective-permute-start.29 = (bf16[128,1280]{1,0:T(8,128)(2,1)S(1)}, bf16[128,1280]{1,0:T(8,128)(2,1)S(1)}, u32[]{:S(2)}, u32[]{:S(2)}) collective-permute-start(bf16[128,1280]{1,0:T(8,128)(2,1)S(1)} %slice.173), channel_id=1, source_target_pairs={{0,16},{1,17},{2,18},{3,19},{4,20},{5,21},{6,22},{7,23},{8,24},{9,... | collective-permute-start | bytes 983048 | tf_op jit(solution)/shard_map/ppermute | solution.py:57
  176.2 14.8 %collective-permute-start.33 = (bf16[128,2048]{1,0:T(8,128)(2,1)S(1)}, bf16[128,2048]{1,0:T(8,128)(2,1)S(1)}, u32[]{:S(2)}, u32[]{:S(2)}) collective-permute-start(bf16[128,2048]{1,0:T(8,128)(2,1)S(1)} %slice.177), channel_id=1, source_target_pairs={{0,1},{1,0},{2,3},{3,2},{4,5},{5,4},{6,7},{7,6},{8,9},{9,8},{10,11... | collective-permute-start | bytes 1572872 | tf_op jit(solution)/shard_map/ppermute | solution.py:57
  176.4 26.9 %collective-permute-start.44 = (bf16[16,7680]{1,0:T(8,128)(2,1)S(1)}, bf16[16,7680]{1,0:T(8,128)(2,1)S(1)}, u32[]{:S(2)}, u32[]{:S(2)}) collective-permute-start(bf16[16,7680]{1,0:T(8,128)(2,1)S(1)} %get-tuple-element.129), channel_id=1, source_target_pairs={{0,6},{1,7},{2,4},{3,5},{4,2},{5,3},{6,0},{7,1},{8,14},{9,15},{10,... | collective-permute-start | bytes 737288 | tf_op jit(solution)/shard_map/ppermute | solution.py:57
  181.7 22.1 %collective-permute-start.43 = (bf16[16,7680]{1,0:T(8,128)(2,1)S(1)}, bf16[16,7680]{1,0:T(8,128)(2,1)S(1)}, u32[]{:S(2)}, u32[]{:S(2)}) collective-permute-start(bf16[16,7680]{1,0:T(8,128)(2,1)S(1)} %get-tuple-element.130), channel_id=1, source_target_pairs={{0,4},{1,5},{2,6},{3,7},{4,0},{5,1},{6,2},{7,3},{8,12},{9,13},{10,... | collective-permute-start | bytes 737288 | tf_op jit(solution)/shard_map/ppermute | solution.py:57
  181.7 22.1 %collective-permute-start.42 = (bf16[16,7680]{1,0:T(8,128)(2,1)S(1)}, bf16[16,7680]{1,0:T(8,128)(2,1)S(1)}, u32[]{:S(2)}, u32[]{:S(2)}) collective-permute-start(bf16[16,7680]{1,0:T(8,128)(2,1)S(1)} %get-tuple-element.128), channel_id=1, source_target_pairs={{0,2},{1,3},{2,0},{3,1},{4,6},{5,7},{6,4},{7,5},{8,10},{9,11},{10,... | collective-permute-start | bytes 737288 | tf_op jit(solution)/shard_map/ppermute | solution.py:57
  184.9 9.0 %collective-permute-start.30 = (bf16[64,1280]{1,0:T(8,128)(2,1)S(1)}, bf16[64,1280]{1,0:T(8,128)(2,1)S(1)}, u32[]{:S(2)}, u32[]{:S(2)}) collective-permute-start(bf16[64,1280]{1,0:T(8,128)(2,1)S(1)} %slice.175), channel_id=1, source_target_pairs={{0,1},{1,0},{2,3},{3,2},{4,5},{5,4},{6,7},{7,6},{8,9},{9,8},{10,11... | collective-permute-start | bytes 491528 | tf_op jit(solution)/shard_map/ppermute | solution.py:57
  191.2 6.9 %collective-permute-start.34 = (bf16[64,2048]{1,0:T(8,128)(2,1)S(1)}, bf16[64,2048]{1,0:T(8,128)(2,1)S(1)}, u32[]{:S(2)}, u32[]{:S(2)}) collective-permute-start(bf16[64,2048]{1,0:T(8,128)(2,1)S(1)} %slice.179), channel_id=1, source_target_pairs={{0,16},{1,17},{2,18},{3,19},{4,20},{5,21},{6,22},{7,23},{8,24},{9,... | collective-permute-start | bytes 786440 | tf_op jit(solution)/shard_map/ppermute | solution.py:57
  198.3 8.2 %collective-permute-start.37 = (bf16[16,3328]{1,0:T(8,128)(2,1)S(1)}, bf16[16,3328]{1,0:T(8,128)(2,1)S(1)}, u32[]{:S(2)}, u32[]{:S(2)}) collective-permute-start(bf16[16,3328]{1,0:T(8,128)(2,1)S(1)} %get-tuple-element.136), channel_id=1, source_target_pairs={{0,6},{1,7},{2,4},{3,5},{4,2},{5,3},{6,0},{7,1},{8,14},{9,15},{10,... | collective-permute-start | bytes 319496 | tf_op jit(solution)/shard_map/ppermute | solution.py:57
  202.6 9.1 %collective-permute-start.36 = (bf16[16,3328]{1,0:T(8,128)(2,1)S(1)}, bf16[16,3328]{1,0:T(8,128)(2,1)S(1)}, u32[]{:S(2)}, u32[]{:S(2)}) collective-permute-start(bf16[16,3328]{1,0:T(8,128)(2,1)S(1)} %get-tuple-element.137), channel_id=1, source_target_pairs={{0,4},{1,5},{2,6},{3,7},{4,0},{5,1},{6,2},{7,3},{8,12},{9,13},{10,... | collective-permute-start | bytes 319496 | tf_op jit(solution)/shard_map/ppermute | solution.py:57
  203.3 8.4 %collective-permute-start.35 = (bf16[16,3328]{1,0:T(8,128)(2,1)S(1)}, bf16[16,3328]{1,0:T(8,128)(2,1)S(1)}, u32[]{:S(2)}, u32[]{:S(2)}) collective-permute-start(bf16[16,3328]{1,0:T(8,128)(2,1)S(1)} %get-tuple-element.135), channel_id=1, source_target_pairs={{0,2},{1,3},{2,0},{3,1},{4,6},{5,7},{6,4},{7,5},{8,10},{9,11},{10,... | collective-permute-start | bytes 319496 | tf_op jit(solution)/shard_map/ppermute | solution.py:57
  (3 other events, 2.5 us)
